TPU v7x, 256 devices: a whole 4x4x8 slice. The times are simulated.
256 devices in a mesh: clip: 32 (over x, z_hi, core), seq: 8 (over z_lo, y).
Axes of the slice: x: 4, y: 4, z: 8 (z_hi: 4, z_lo: 2; z = z_hi * 2 + z_lo), core: 2. Of those that a mesh axis runs over, the one named last changes fastest.
Arguments:
- enc_terms: bfloat16 [32, 8, 128, 4096], P('clip', 'seq'), may hold values from -4 to 4
- enc_resid: bfloat16 [32, 128, 4096], P('clip'), may hold values from -6 to 6
- norm_gain: float32 [4096], replicated, may hold values from 0.1 to 1.9
- key_weight: bfloat16 [4096, 5120], P('clip', 'seq'), may hold values from -0.09375 to 0.09375
- value_weight: bfloat16 [4096, 5120], P('clip', 'seq'), may hold values from -0.09375 to 0.09375
- queries: bfloat16 [32, 1024, 5120], P('clip', 'seq'), may hold values from -6 to 6
- out_grad: bfloat16 [32, 1024, 5120], P('clip', 'seq'), may hold values from -6 to 6
Outputs:
- query_grad: bfloat16 [32, 1024, 5120], P('clip', 'seq')
- key_weight_grad: float32 [4096, 5120], P('clip', 'seq')
- value_weight_grad: float32 [4096, 5120], P('clip', 'seq')
All inputs are finite; a program needn't handle non-finite values.
Results may differ from a plain program's by a relative error of at most 0.034.
Values may be sent and summed in bfloat16 or wider, within the bound.
A program may use at most 64 MiB of HBM per device.

v0:
```python
import jax
import jax.numpy as jnp
from jax import lax
from jax.sharding import PartitionSpec as P

HEAD_DIM = 128


def normalize(hidden, gain):
    mean_sq = jnp.mean(hidden * hidden, axis=-1, keepdims=True)
    return (hidden * lax.rsqrt(mean_sq + 1e-06) * gain).astype(jnp.bfloat16)


def attend(query_rows, grad_rows, keys, values):
    count = query_rows.shape[0]
    heads = keys.shape[1] // HEAD_DIM
    scale = HEAD_DIM ** (-0.5)
    q_heads = query_rows.reshape(count, heads, HEAD_DIM)
    g_heads = grad_rows.reshape(count, heads, HEAD_DIM)
    k_heads = keys.reshape(keys.shape[0], heads, HEAD_DIM)
    v_heads = values.reshape(values.shape[0], heads, HEAD_DIM)
    scores = (
        jnp.einsum("nhd,thd->hnt", q_heads, k_heads, preferred_element_type=jnp.float32) * scale
    )
    expo = jnp.exp(scores)
    probs = expo / jnp.sum(expo, axis=-1, keepdims=True)
    probs_b = probs.astype(jnp.bfloat16)
    attn = jnp.einsum("hnt,thd->nhd", probs_b, v_heads, preferred_element_type=jnp.float32)
    delta = jnp.sum(g_heads.astype(jnp.float32) * attn, axis=-1)
    dprobs = jnp.einsum("nhd,thd->hnt", g_heads, v_heads, preferred_element_type=jnp.float32)
    dscores = (probs * (dprobs - jnp.transpose(delta)[:, :, None])).astype(jnp.bfloat16)
    query_grad = (
        jnp.einsum("hnt,thd->nhd", dscores, k_heads, preferred_element_type=jnp.float32) * scale
    )
    key_grad = (
        jnp.einsum("hnt,nhd->thd", dscores, q_heads, preferred_element_type=jnp.float32) * scale
    )
    val_grad = jnp.einsum("hnt,nhd->thd", probs_b, g_heads, preferred_element_type=jnp.float32)
    width = heads * HEAD_DIM
    return (
        query_grad.astype(jnp.bfloat16).reshape(count, width),
        key_grad.reshape(keys.shape[0], width),
        val_grad.reshape(keys.shape[0], width),
    )


def on_device(enc_terms, enc_resid, norm_gain, key_weight, value_weight, queries, out_grad):
    partial_terms = enc_terms[0, 0].astype(jnp.float32)
    resid_rows = enc_resid[0].astype(jnp.float32)
    enc_sum = lax.psum(partial_terms.astype(jnp.bfloat16), "seq").astype(jnp.float32)
    text = normalize(resid_rows + enc_sum, norm_gain)
    local_width = key_weight.shape[1]
    columns = text
    key_acc = jnp.dot(
        columns,
        lax.all_gather(key_weight, "clip", axis=0, tiled=True),
        preferred_element_type=jnp.float32,
    )
    val_acc = jnp.dot(
        columns,
        lax.all_gather(value_weight, "clip", axis=0, tiled=True),
        preferred_element_type=jnp.float32,
    )
    keys_local = key_acc.astype(jnp.bfloat16)
    values_local = val_acc.astype(jnp.bfloat16)
    keys_all, values_all = (
        lax.all_gather(keys_local, "seq", axis=1, tiled=True),
        lax.all_gather(values_local, "seq", axis=1, tiled=True),
    )
    query_grad, key_part, val_part = attend(queries[0], out_grad[0], keys_all, values_all)
    key_grad, val_grad = (
        lax.psum_scatter(
            key_part.astype(jnp.bfloat16), "seq", scatter_dimension=1, tiled=True
        ).astype(jnp.float32),
        lax.psum_scatter(
            val_part.astype(jnp.bfloat16), "seq", scatter_dimension=1, tiled=True
        ).astype(jnp.float32),
    )
    both_grads = jnp.concatenate(
        (key_grad.astype(jnp.bfloat16), val_grad.astype(jnp.bfloat16)), axis=1
    )
    columns = text
    summed = lax.psum_scatter(
        lax.dot_general(
            columns, both_grads, (((0,), (0,)), ((), ())), preferred_element_type=jnp.float32
        ).astype(jnp.bfloat16),
        "clip",
        scatter_dimension=0,
        tiled=True,
    ).astype(jnp.float32)
    return (query_grad[None], summed[:, :local_width], summed[:, local_width:])


def solution(mesh):
    in_specs = (
        P("clip", "seq", None, None),
        P("clip", None, None),
        P(),
        P("clip", "seq"),
        P("clip", "seq"),
        P("clip", "seq", None),
        P("clip", "seq", None),
    )
    out_specs = (P("clip", "seq", None), P("clip", "seq"), P("clip", "seq"))
    return jax.shard_map(
        on_device, mesh=mesh, in_specs=in_specs, out_specs=out_specs, check_vma=False
    )
```

profile of v0, /device:TPU:1, one launch (start us, length us, event | category | flops | bytes accessed | tf_op | source)
XLA Modules:
  0.0 478.1 jit_solution(17047622027603215484)
XLA Ops:
  8.0 0.0 copy-start.2
  8.0 0.0 copy-start.8
  8.0 0.0 all-reduce.2.cloned.1.call-start
  8.1 0.7 all-reduce.2.cloned.1.call-update
  8.8 0.0 all-gather.5.cloned.1.call-start
  8.8 0.5 all-gather.5.cloned.1.call-update
  9.3 0.0 all-gather.9.cloned.1.call-start
  9.4 0.5 all-gather.9.cloned.1.call-update
  9.9 0.0 all-gather.7.cloned.1.call-start
  10.0 88.4 %all-reduce.2.cloned.1.call-done = bf16[128,4096]{1,0:T(8,128)(2,1)} async-done(((bf16[128,4096]{1,0:T(8,128)(2,1)}), bf16[128,4096]{1,0:T(8,128)(2,1)}) %all-reduce.2.cloned.1.call-update) | async-done | bytes 1048592 | tf_op jit(solution)/shard_map/psum | solution.py:50
  98.3 0.0 copy-done.2
  98.3 0.0 copy-start.3
  98.3 1.7 multiply_reduce_fusion
  100.1 0.0 copy-done.8
  100.1 0.0 copy-done.3
  100.1 0.4 multiply_convert_fusion.2
  100.5 0.0 all-gather.5.cloned.1.call-done
  100.5 4.2 convolution_convert_fusion.3
  104.7 0.0 all-gather.7.cloned.1.call-update
  104.7 0.0 copy-start.5
  104.8 0.0 all-gather.11.cloned.1.call-start
  104.8 43.5 %all-gather.9.cloned.1.call-done = bf16[4096,640]{1,0:T(8,128)(2,1)} async-done(((bf16[128,640]{1,0:T(8,128)(2,1)}), bf16[4096,640]{1,0:T(8,128)(2,1)}) %all-gather.9.cloned.1.call-update) | async-done | bytes 5242896 | tf_op jit(solution)/shard_map/all_gather | solution.py:61
  148.3 4.1 convolution_convert_fusion.2
  152.5 0.0 all-gather.11.cloned.1.call-update
  152.5 0.0 reduce-scatter.4.cloned.1.call-start
  152.5 0.0 copy-done.5
  152.6 1.4 copy.46
  154.0 2.4 copy.26
  156.4 28.3 %all-gather.7.cloned.1.call-done = bf16[128,5120]{1,0:T(8,128)(2,1)} async-done(((bf16[128,640]{1,0:T(8,128)(2,1)}), bf16[128,5120]{1,0:T(8,128)(2,1)}) %all-gather.7.cloned.1.call-update) | async-done | bytes 1310736 | tf_op jit(solution)/shard_map/all_gather | solution.py:67
  184.8 1.8 copy.45
  186.5 3.5 bitcast_reduce_fusion
  190.1 38.8 %all-gather.11.cloned.1.call-done = bf16[128,5120]{1,0:T(8,128)(2,1)} async-done(((bf16[128,640]{1,0:T(8,128)(2,1)}), bf16[128,5120]{1,0:T(8,128)(2,1)}) %all-gather.11.cloned.1.call-update) | async-done | bytes 1310736 | tf_op jit(solution)/shard_map/all_gather | solution.py:68
  228.9 2.4 copy.47
  231.3 0.0 copy-start.4
  231.3 0.0 copy-start.6
  231.3 0.0 copy-start.7
  231.3 3.5 fusion.1
  234.8 0.0 copy-done.4
  234.8 0.1 copy-done.6
  235.0 0.4 copy-done.7
  235.4 0.0 copy-start
  235.4 1.0 fusion
  236.3 0.0 copy-start.1
  236.4 1.0 copy-done.1
  237.4 0.0 copy-done
  237.4 2.1 fusion.2
  239.5 2.4 copy.36
  242.0 0.0 reduce-scatter.4.cloned.1.call-update
  242.0 0.0 reduce-scatter.6.cloned.1.call-start
  242.0 4.2 convolution_convert_fusion.1
  246.3 0.0 reduce-scatter.6.cloned.1.call-update
  246.3 0.0 reduce-scatter.8.cloned.1.call-start
  246.4 38.3 %reduce-scatter.4.cloned.1.call-done = bf16[128,640]{0,1:T(8,128)(2,1)} async-done(((bf16[128,5120]{0,1:T(8,128)(2,1)}), bf16[128,640]{0,1:T(8,128)(2,1)}) %reduce-scatter.4.cloned.1.call-update) | async-done | bytes 163856 | tf_op jit(solution)/shard_map/reduce_scatter | solution.py:72
  284.6 43.8 %reduce-scatter.6.cloned.1.call-done = bf16[128,640]{0,1:T(8,128)(2,1)} async-done(((bf16[128,5120]{0,1:T(8,128)(2,1)}), bf16[128,640]{0,1:T(8,128)(2,1)}) %reduce-scatter.6.cloned.1.call-update) | async-done | bytes 163856 | tf_op jit(solution)/shard_map/reduce_scatter | solution.py:75
  328.5 6.5 %convolution_convert_fusion = bf16[4096,1280]{1,0:T(8,128)(2,1)} fusion(bf16[128,4096]{1,0:T(8,128)(2,1)S(1)} %multiply_convert_fusion.2, bf16[128,640]{0,1:T(8,128)(2,1)} %reduce-scatter.6.cloned.1.call-done, bf16[128,640]{0,1:T(8,128)(2,1)} %reduce-scatter.4.cloned.1.call-done), kind=kOutput, calls=%fused_computation | convolution fusion | flops 1348075520 | bytes 11862016 | tf_op jit(solution)/shard_map/dot_general | solution.py:84
  335.0 0.0 reduce-scatter.8.cloned.1.call-update
  335.0 2.9 multiply_convert_fusion.1
  337.9 2.4 copy.38
  340.3 128.5 %reduce-scatter.8.cloned.1.call-done = bf16[128,1280]{1,0:T(8,128)(2,1)} async-done(((bf16[4096,1280]{1,0:T(8,128)(2,1)}), bf16[128,1280]{1,0:T(8,128)(2,1)}) %reduce-scatter.8.cloned.1.call-update) | async-done | bytes 327696 | tf_op jit(solution)/shard_map/reduce_scatter | solution.py:83
  468.8 1.9 fusion.10
  (1 shorter events, 0.0 us)
Async XLA Ops:
  8.0 90.3 %copy-start.2 = (bf16[1,128,4096]{2,1,0:T(8,128)(2,1)S(1)}, bf16[1,128,4096]{2,1,0:T(8,128)(2,1)}, u32[]{:S(2)}) copy-start(bf16[1,128,4096]{2,1,0:T(8,128)(2,1)} %param.8) | copy-start | bytes 3145732
  8.0 92.1 %copy-start.8 = (f32[4096]{0:T(1024)S(1)}, f32[4096]{0:T(1024)}, u32[]{:S(2)}) copy-start(f32[4096]{0:T(1024)} %param.9) | copy-start | bytes 49156
  8.0 90.3 %all-reduce.2.cloned.1.call-start = ((), (), s32[]{:S(2)}) async-start(), calls=%async_computation.3 | async-start | bytes 2097152 | tf_op jit(solution)/shard_map/psum | solution.py:50
  8.8 91.8 %all-gather.5.cloned.1.call-start = ((), (), s32[]{:S(2)}) async-start(), calls=%async_computation.4 | async-start | bytes 5406720 | tf_op jit(solution)/shard_map/all_gather | solution.py:56
  9.3 139.0 %all-gather.9.cloned.1.call-start = ((), (), s32[]{:S(2)}) async-start(), calls=%async_computation.6 | async-start | bytes 5406720 | tf_op jit(solution)/shard_map/all_gather | solution.py:61
  9.9 174.9 %all-gather.7.cloned.1.call-start = ((), (), s32[]{:S(2)}) async-start(), calls=%async_computation.5 | async-start | bytes 1474560 | tf_op jit(solution)/shard_map/all_gather | solution.py:67
  98.3 1.8 copy-start.3
  104.7 47.8 %copy-start.5 = (bf16[1,128,5120]{2,1,0:T(8,128)(2,1)S(1)}, bf16[1,128,5120]{2,1,0:T(8,128)(2,1)}, u32[]{:S(2)}) copy-start(bf16[1,128,5120]{2,1,0:T(8,128)(2,1)} %param.12) | copy-start | bytes 3932164
  104.8 124.1 %all-gather.11.cloned.1.call-start = ((), (), s32[]{:S(2)}) async-start(), calls=%async_computation.7 | async-start | bytes 1474560 | tf_op jit(solution)/shard_map/all_gather | solution.py:68
  152.5 132.1 %reduce-scatter.4.cloned.1.call-start = ((), (), s32[]{:S(2)}) async-start(), calls=%async_computation.8 | async-start | bytes 1474560 | tf_op jit(solution)/shard_map/reduce_scatter | solution.py:72
  231.3 3.5 copy-start.4
  231.3 3.7 copy-start.6
  231.3 4.1 copy-start.7
  235.4 2.0 copy-start
  236.3 1.1 copy-start.1
  242.0 86.5 %reduce-scatter.6.cloned.1.call-start = ((), (), s32[]{:S(2)}) async-start(), calls=%async_computation.9 | async-start | bytes 1474560 | tf_op jit(solution)/shard_map/reduce_scatter | solution.py:75
  246.3 222.5 %reduce-scatter.8.cloned.1.call-start = ((), (), s32[]{:S(2)}) async-start(), calls=%async_computation.10 | async-start | bytes 10813440 | tf_op jit(solution)/shard_map/reduce_scatter | solution.py:83
Sparse Core Ops, SparseCore 0:
  11.5 86.7 all-reduce.1
  242.1 42.4 reduce-scatter.3
  287.2 41.2 reduce-scatter.5
Sparse Core Ops, SparseCore 1:
  11.8 71.2 all-gather.4
  85.4 62.9 all-gather.8
  150.6 34.1 all-gather.6
  187.2 41.6 all-gather.10
  335.1 133.7 reduce-scatter.7
where the time goes:
time: 479 us; the launch traced here: 478 us
  waiting for transfers between devices  411 us (86%)
  matrix products  32.2 us (7%)
  local copies, waits for them, and re-layouts  16.4 us (3%)
  between operations  15.6 us (3%)
    reduce_scatter x1, waiting for transfers between devices, on_device(): lax.psum_scatter(lax.dot_general(columns, both_grads, (((0,), (0,)), ((),...  129 us
    psum x1, waiting for transfers between devices, on_device(): lax.psum(partial_terms.astype(jnp.bfloat16), 'seq').astype(jnp.float32)  88.4 us
    reduce_scatter x1, waiting for transfers between devices, on_device(): lax.psum_scatter(val_part.astype(jnp.bfloat16), 'seq', scatter_dimension=...  43.8 us
    all_gather x1, waiting for transfers between devices, on_device(): lax.all_gather(value_weight, 'clip', axis=0, tiled=True)  43.5 us
    all_gather x1, waiting for transfers between devices, on_device(): lax.all_gather(values_local, 'seq', axis=1, tiled=True)  38.8 us
    reduce_scatter x1, waiting for transfers between devices, on_device(): lax.psum_scatter(key_part.astype(jnp.bfloat16), 'seq', scatter_dimension=...  38.3 us
    all_gather x1, waiting for transfers between devices, on_device(): lax.all_gather(keys_local, 'seq', axis=1, tiled=True)  28.3 us
  transfers between devices with their start and end apart: 8, of which 7 were waited for; matrix products, arithmetic and copies ran while one was open for 6% of the time, Pallas kernels for 0%

commit v1 on v0

v1 whole, which is shorter than its diff:
```python
import jax
import jax.numpy as jnp
from jax import lax
from jax.experimental import pallas as pl
from jax.experimental.pallas import tpu as pltpu
from jax.sharding import PartitionSpec as P

MESH = pl.DeviceIdType.MESH
HEAD = 128
F32 = jnp.float32
BF16 = jnp.bfloat16


def dot(a, b, ca, cb):
    return lax.dot_general(a, b, (((ca,), (cb,)), ((), ())), preferred_element_type=F32)


def each(start, stop, body):
    lax.fori_loop(start, stop, lambda i, c: (body(i), c)[1], 0)


def device(x, z, k, l, y):
    return ((x * 4 + z) * 2 + k, l * 4 + y)


def kernel(
    enc, resid, gain, key_w, val_w, queries, grads,
    out_q, out_k, out_v,
    enc_buf, res_buf, text16, text, w_own, w_all, kv_part, kv_recv, kv, q_buf, g_buf, qg_buf,
    pg_send, pg_own, pg_recv, gr_own, gr_all, dw_part, dw_recv,
    loc, e_s, e_r, t1_s, t1_r, t2_s, t2_r, t3_s, t3_r, w_s, w_r, kv_s, kv_r, kx_s, kx_r,
    qg_s, qg_r, px_s, px_r, oq_s, oq_r, ga_s, ga_r, dw_s, dw_r,
):
    clip, seq = lax.axis_index("clip"), lax.axis_index("seq")
    x, z, k = lax.div(clip, 8), lax.rem(lax.div(clip, 2), 4), lax.rem(clip, 2)
    l, y = lax.div(seq, 4), lax.rem(seq, 4)
    el, ek = 1 - l, 1 - k

    def seq_dev(j):
        return device(x, z, k, lax.div(j, 4), lax.rem(j, 4))

    def row_dev(e):
        return device(x, lax.div(e, 2), lax.rem(e, 2), l, y)

    def clip_dev(e):
        return device(lax.rem(e, 4), z, lax.div(e, 4), l, y)

    my_row, my_clip = z * 2 + k, k * 4 + x

    def remote(src, dst, s, r, where):
        return pltpu.make_async_remote_copy(
            src_ref=src, dst_ref=dst, send_sem=s, recv_sem=r, device_id=where, device_id_type=MESH
        )

    def local(src, dst, i):
        return pltpu.make_async_copy(src, dst, loc.at[i])

    local(enc.at[0, 0, pl.ds(pl.multiple_of(seq * 16, 16), 16)], enc_buf.at[seq], 0).start()
    local(resid.at[0, pl.ds(pl.multiple_of(seq * 16, 16), 16)], res_buf, 1).start()
    local(key_w, w_own.at[0], 2).start()
    local(val_w, w_own.at[1], 3).start()

    def own_qg(i, l2):
        src, dst = ((queries, q_buf), (grads, g_buf))[i]
        return local(
            src.at[0, :, pl.ds(pl.multiple_of((l2 * 4 + y) * 640, 128), 640)],
            dst.at[l2, pl.ds(pl.multiple_of(y * 128, 128), 128)],
            4 + 2 * i + l2,
        )

    for i in range(2):
        for l2 in range(2):
            own_qg(i, l2).start()

    bar = pltpu.get_barrier_semaphore()

    def greet(where):
        pl.semaphore_signal(bar, inc=1, device_id=where, device_id_type=MESH)

    each(1, 8, lambda o: greet(seq_dev(lax.rem(seq + o, 8))))
    each(1, 8, lambda o: greet(row_dev(lax.rem(my_row + o, 8))))
    each(1, 8, lambda o: greet(clip_dev(lax.rem(my_clip + o, 8))))
    pl.semaphore_wait(bar, 21)

    def enc_copy(j, slot):
        return remote(
            enc.at[0, 0, pl.ds(pl.multiple_of(j * 16, 16), 16)],
            enc_buf.at[slot], e_s.at[j], e_r.at[slot], seq_dev(j),
        )

    each(1, 8, lambda o: enc_copy(lax.rem(seq + o, 8), seq).start())

    local(key_w, w_own.at[0], 2).wait()
    local(val_w, w_own.at[1], 3).wait()

    def w_copy(e, slot):
        return remote(
            w_own.at[lax.rem(e, 2)], w_all.at[slot], w_s.at[e], w_r.at[slot], row_dev(e)
        )

    each(1, 8, lambda o: w_copy(lax.rem(my_row + o, 8), my_row).start())
    local(w_own.at[k], w_all.at[my_row], 8).start()

    local(enc.at[0, 0, pl.ds(pl.multiple_of(seq * 16, 16), 16)], enc_buf.at[seq], 0).wait()
    local(resid.at[0, pl.ds(pl.multiple_of(seq * 16, 16), 16)], res_buf, 1).wait()

    def enc_wait(o):
        j = lax.rem(seq + o, 8)
        enc_copy(j, j).wait_recv()

    each(1, 8, enc_wait)
    hidden = []
    total = jnp.zeros((16, 1), F32)
    for b in range(4):
        cols = pl.ds(b * 1024, 1024)
        h = enc_buf[0, :, cols].astype(F32)
        for s in range(1, 8):
            h = h + enc_buf[s, :, cols].astype(F32)
        h = h + res_buf[:, cols].astype(F32)
        total = total + jnp.sum(h * h, axis=1, keepdims=True)
        hidden.append(h)
    inv = lax.rsqrt(total * (1.0 / 4096.0) + 1e-06)
    for b in range(4):
        cols = pl.ds(b * 1024, 1024)
        text16[b] = (hidden[b] * inv * gain[:, cols]).astype(BF16)

    rows16 = pl.ds(pl.multiple_of(seq * 16, 16), 16)

    def t1_copy(x2, slot):
        return remote(
            text16.at[x2], text.at[k, slot, rows16], t1_s.at[x2], t1_r.at[slot], device(x2, z, k, l, y)
        )

    each(1, 4, lambda o: t1_copy(lax.rem(x + o, 4), x).start())
    local(text16.at[x], text.at[k, x, rows16], 9).start()
    local(text16.at[x], text.at[k, x, rows16], 9).wait()

    def t1_wait(o):
        x2 = lax.rem(x + o, 4)
        t1_copy(x2, x2).wait_recv()

    each(1, 4, t1_wait)

    def t2_copy(j, slot):
        part = text.at[k, :, pl.ds(pl.multiple_of(slot * 16, 16), 16)]
        return remote(part, part, t2_s.at[j], t2_r.at[slot], seq_dev(j))

    each(1, 8, lambda o: t2_copy(lax.rem(seq + o, 8), seq).start())

    def qg_copy(i, l2, y2, slot):
        src, dst = ((queries, q_buf), (grads, g_buf))[i]
        return remote(
            src.at[0, :, pl.ds(pl.multiple_of((l2 * 4 + y2) * 640, 128), 640)],
            dst.at[l2, pl.ds(pl.multiple_of(slot * 128, 128), 128)],
            qg_s.at[2 * i + l2, y2], qg_r.at[2 * i + l2, slot], device(x, z, k, l, y2),
        )

    def t2_wait(o):
        j = lax.rem(seq + o, 8)
        t2_copy(j, j).wait_recv()

    each(1, 8, t2_wait)

    t3 = remote(text.at[k], text.at[k], t3_s.at[0], t3_r.at[0], device(x, z, ek, l, y))
    t3.start()

    def qg_start(o):
        y2 = lax.rem(y + o, 4)
        for i in range(2):
            for l2 in range(2):
                qg_copy(i, l2, y2, y).start()

    each(1, 4, qg_start)

    local(w_own.at[k], w_all.at[my_row], 8).wait()

    def w_wait(o):
        e = lax.rem(my_row + o, 8)
        w_copy(e, e).wait_recv()

    each(1, 8, w_wait)

    def kv_copy(e, slot):
        a, b = lax.div(e, 4), lax.rem(e, 4)
        c, d = lax.div(slot, 4), lax.rem(slot, 4)
        return remote(
            kv_part.at[a, b], kv_recv.at[c, d], kv_s.at[e], kv_r.at[slot], clip_dev(e)
        )

    def project(core):
        t = text[core].reshape(512, 1024)
        for n in (0, 256, 512):
            size = min(256, 640 - n)
            acc = dot(t, w_all[:, :, n : n + size].reshape(1024, size), 1, 0)
            kv_part[core, :, :, n : n + size] = acc.astype(BF16).reshape(4, 128, size)

    project(k)
    each(1, 4, lambda o: kv_copy(k * 4 + lax.rem(x + o, 4), my_clip).start())
    local(kv_part.at[k, x], kv_recv.at[k, x], 10).start()
    remote(text.at[ek], text.at[ek], t3_s.at[0], t3_r.at[0], device(x, z, ek, l, y)).wait_recv()
    project(ek)
    each(0, 4, lambda o: kv_copy(ek * 4 + lax.rem(x + o, 4), my_clip).start())
    local(kv_part.at[k, x], kv_recv.at[k, x], 10).wait()

    def kv_wait(o):
        e = lax.rem(my_clip + o, 8)
        kv_copy(e, e).wait_recv()

    each(1, 8, kv_wait)
    for i in range(2):
        acc = kv_recv[i, 0].astype(F32)
        for b in range(1, 4):
            acc = acc + kv_recv[i, b].astype(F32)
        kv[l, i] = acc.astype(BF16)

    def kx_copy(slot):
        return remote(kv.at[slot], kv.at[slot], kx_s.at[0], kx_r.at[0], device(x, z, k, el, y))

    kx_copy(l).start()

    scale = HEAD ** (-0.5)

    def qg_wait(l2):
        def from_y(o):
            y2 = lax.rem(y + o, 4)
            for i in range(2):
                qg_copy(i, l2, y2, y2).wait_recv()

        for i in range(2):
            own_qg(i, l2).wait()
        each(1, 4, from_y)

    def head(l2, c, keep):
        cols = pl.ds(pl.multiple_of(c * HEAD, HEAD), HEAD)
        qh, gh = q_buf[l2, :, cols], g_buf[l2, :, cols]
        kh, vh = kv[l2, 0, :, cols], kv[l2, 1, :, cols]
        e = jnp.exp(dot(kh, qh, 1, 1) * scale)
        probs = e * (1.0 / jnp.sum(e, axis=0, keepdims=True))
        probs_b = probs.astype(BF16)
        dprobs = dot(vh, gh, 1, 1)
        delta = jnp.sum(probs_b.astype(F32) * dprobs, axis=0, keepdims=True)
        ds = (probs * (dprobs - delta)).astype(BF16)
        qg_buf[l2, :, cols] = (dot(ds, kh, 0, 0) * scale).astype(BF16)
        keep[0, :, cols] = (dot(ds, qh, 1, 0) * scale).astype(keep.dtype)
        keep[1, :, cols] = dot(probs_b, gh, 1, 0).astype(keep.dtype)

    def oq_copy(l2, y2, slot):
        return remote(
            qg_buf.at[l2, pl.ds(pl.multiple_of(y2 * 128, 128), 128)],
            out_q.at[0, :, pl.ds(pl.multiple_of((l2 * 4 + slot) * 640, 128), 640)],
            oq_s.at[l2, y2], oq_r.at[l2, slot], device(x, z, k, l, y2),
        )

    def oq_own(l2):
        return local(
            qg_buf.at[l2, pl.ds(pl.multiple_of(y * 128, 128), 128)],
            out_q.at[0, :, pl.ds(pl.multiple_of((l2 * 4 + y) * 640, 128), 640)],
            11 + l2,
        )

    qg_wait(0)
    qg_wait(1)
    kx_copy(el).wait_recv()
    each(0, 5, lambda c: head(el, c, pg_send))

    def px_copy():
        return remote(pg_send, pg_recv, px_s.at[0], px_r.at[0], device(x, z, k, el, y))

    px_copy().start()
    each(0, 5, lambda c: head(l, c, pg_own))
    px_copy().wait_recv()
    gr_own[...] = (pg_own[...] + pg_recv[...].astype(F32)).astype(BF16)

    def ga_copy(e, slot):
        c, d = lax.div(slot, 4), lax.rem(slot, 4)
        return remote(
            gr_own.at[lax.div(e, 4)], gr_all.at[c, d], ga_s.at[e], ga_r.at[slot], clip_dev(e)
        )

    each(1, 8, lambda o: ga_copy(lax.rem(my_clip + o, 8), my_clip).start())
    local(gr_own.at[k], gr_all.at[k, x], 13).start()

    def oq_start(o):
        for l2 in range(2):
            oq_copy(l2, lax.rem(y + o, 4), y).start()

    each(1, 4, oq_start)
    for l2 in range(2):
        oq_own(l2).start()

    local(gr_own.at[k], gr_all.at[k, x], 13).wait()

    def ga_wait(o):
        e = lax.rem(my_clip + o, 8)
        ga_copy(e, e).wait_recv()

    each(1, 8, ga_wait)

    def dw_copy(e, slot):
        c, d = lax.rem(slot, 2), lax.div(slot, 2)
        return remote(dw_part.at[e], dw_recv.at[c, d], dw_s.at[e], dw_r.at[slot], row_dev(e))

    def dw_step(o):
        z2 = lax.rem(z + o, 4)
        cols = pl.ds(pl.multiple_of(z2 * 256, 256), 256)
        t = text[:, :, :, cols].reshape(1024, 256)
        for n in (0, 256, 512):
            size = min(256, 640 - n)
            acc = dot(t, gr_all[:, :, :, n : n + size].reshape(1024, size), 0, 0)
            dw_part[pl.ds(z2 * 2, 2), :, n : n + size] = acc.astype(BF16).reshape(2, 128, size)

    def dw_send(o):
        dw_step(o)
        z2 = lax.rem(z + o, 4)
        for k2 in range(2):
            dw_copy(z2 * 2 + k2, my_row).start()

    each(1, 4, dw_send)
    dw_step(0)
    dw_copy(z * 2 + ek, my_row).start()
    local(dw_part.at[my_row], dw_recv.at[k, z], 14).start()
    local(dw_part.at[my_row], dw_recv.at[k, z], 14).wait()

    def dw_wait(o):
        e = lax.rem(my_row + o, 8)
        dw_copy(e, e).wait_recv()

    each(1, 8, dw_wait)
    for i, out in ((0, out_k), (1, out_v)):
        acc = dw_recv[i, 0].astype(F32)
        for b in range(1, 4):
            acc = acc + dw_recv[i, b].astype(F32)
        out[...] = acc

    def oq_wait(o):
        y2 = lax.rem(y + o, 4)
        for l2 in range(2):
            oq_copy(l2, y2, y2).wait_recv()
            oq_copy(l2, y2, y).wait_send()
            for i in range(2):
                qg_copy(i, l2, y2, y).wait_send()

    each(1, 4, oq_wait)
    for l2 in range(2):
        oq_own(l2).wait()

    def send_wait(o):
        j = lax.rem(seq + o, 8)
        enc_copy(j, seq).wait_send()
        t2_copy(j, seq).wait_send()
        e = lax.rem(my_row + o, 8)
        w_copy(e, my_row).wait_send()
        dw_copy(e, my_row).wait_send()
        e = lax.rem(my_clip + o, 8)
        kv_copy(e, my_clip).wait_send()
        ga_copy(e, my_clip).wait_send()

    each(1, 8, send_wait)
    each(1, 4, lambda o: t1_copy(lax.rem(x + o, 4), x).wait_send())
    t3.wait_send()
    kx_copy(l).wait_send()
    px_copy().wait_send()


def on_device(enc_terms, enc_resid, norm_gain, key_weight, value_weight, queries, out_grad):
    any_spec = pl.BlockSpec(memory_space=pl.ANY)
    vmem = pl.BlockSpec(memory_space=pltpu.VMEM)
    dma = pltpu.SemaphoreType.DMA
    scratch = [
        pltpu.VMEM((8, 16, 4096), BF16),
        pltpu.VMEM((16, 4096), BF16),
        pltpu.VMEM((4, 16, 1024), BF16),
        pltpu.VMEM((2, 4, 128, 1024), BF16),
        pltpu.VMEM((2, 128, 640), BF16),
        pltpu.VMEM((8, 128, 640), BF16),
        pltpu.VMEM((2, 4, 128, 640), BF16),
        pltpu.VMEM((2, 4, 128, 640), BF16),
        pltpu.VMEM((2, 2, 128, 640), BF16),
        pltpu.VMEM((2, 512, 640), BF16),
        pltpu.VMEM((2, 512, 640), BF16),
        pltpu.VMEM((2, 512, 640), BF16),
        pltpu.VMEM((2, 128, 640), BF16),
        pltpu.VMEM((2, 128, 640), F32),
        pltpu.VMEM((2, 128, 640), BF16),
        pltpu.VMEM((2, 128, 640), BF16),
        pltpu.VMEM((2, 4, 128, 640), BF16),
        pltpu.VMEM((8, 128, 640), BF16),
        pltpu.VMEM((2, 4, 128, 640), BF16),
        dma((15,)),
        dma((8,)), dma((8,)),
        dma((4,)), dma((4,)),
        dma((8,)), dma((8,)),
        dma((1,)), dma((1,)),
        dma((8,)), dma((8,)),
        dma((8,)), dma((8,)),
        dma((1,)), dma((1,)),
        dma((4, 4)), dma((4, 4)),
        dma((1,)), dma((1,)),
        dma((2, 4)), dma((2, 4)),
        dma((8,)), dma((8,)),
        dma((8,)), dma((8,)),
    ]
    return pl.pallas_call(
        kernel,
        out_shape=(
            jax.ShapeDtypeStruct(queries.shape, BF16),
            jax.ShapeDtypeStruct(key_weight.shape, F32),
            jax.ShapeDtypeStruct(value_weight.shape, F32),
        ),
        in_specs=[any_spec, any_spec, vmem, any_spec, any_spec, any_spec, any_spec],
        out_specs=(any_spec, vmem, vmem),
        scratch_shapes=scratch,
        compiler_params=pltpu.CompilerParams(
            collective_id=0, has_side_effects=True, vmem_limit_bytes=52 * 2**20
        ),
        cost_estimate=pl.CostEstimate(flops=4 * 10**9, bytes_accessed=10**7, transcendentals=655360),
    )(enc_terms, enc_resid, norm_gain.reshape(1, -1), key_weight, value_weight, queries, out_grad)


def solution(mesh):
    in_specs = (
        P("clip", "seq", None, None),
        P("clip", None, None),
        P(),
        P("clip", "seq"),
        P("clip", "seq"),
        P("clip", "seq", None),
        P("clip", "seq", None),
    )
    out_specs = (P("clip", "seq", None), P("clip", "seq"), P("clip", "seq"))
    return jax.shard_map(
        on_device, mesh=mesh, in_specs=in_specs, out_specs=out_specs, check_vma=False
    )
```

time: 479 us -> 163 us (0.34)
  waiting for transfers between devices: 411 us -> 0 us
  Pallas kernels: 0 us -> 156 us
  matrix products: 32.2 us -> 0 us
  between operations: 15.6 us -> 0.65 us
  local copies, waits for them, and re-layouts: 16.4 us -> 6.45 us
    reduce_scatter x3 -> x0, waiting for transfers between devices: 211 us -> none  [the longest x1 129 us: on_device(): lax.psum_scatter(lax.dot_general(columns, both_grads, (((0,), (0,)), ((),...]
    pallas_call x0 -> x1, Pallas kernels: none -> 156 us  [on_device(): pl.pallas_call(kernel, out_shape=(jax.ShapeDtypeStruct(queries.shape, BF1...]
    all_gather x4 -> x0, waiting for transfers between devices: 111 us -> none  [the longest x1 43.5 us: on_device(): lax.all_gather(value_weight, 'clip', axis=0, tiled=True)]
    psum x1 -> x0, waiting for transfers between devices: 88.4 us -> none  [on_device(): lax.psum(partial_terms.astype(jnp.bfloat16), 'seq').astype(jnp.float32)]
    dot_general x9 -> x0, matrix products: 32.2 us -> none  [the longest x1 6.55 us: on_device(): lax.dot_general(columns, both_grads, (((0,), (0,)), ((), ())), preferred_...]
  transfers between devices with their start and end apart: 8 -> 0, of which waited for: 7 -> 0; matrix products, arithmetic and copies ran while one was open for 6% -> 0% of each run, Pallas kernels for 0% -> 0%
where the time goes in v1:
time: 163 us
  Pallas kernels  156 us (96%)
  local copies, waits for them, and re-layouts  6.45 us (4%)
    pallas_call x1, Pallas kernels, on_device(): pl.pallas_call(kernel, out_shape=(jax.ShapeDtypeStruct(queries.shape, BF1...  156 us
    unnamed x9, local copies, waits for them, and re-layouts  6.45 us

profile of v1, /device:TPU:1, one launch (start us, length us, event | category | flops | bytes accessed | tf_op | source)
XLA Modules:
  0.0 163.1 jit_solution(6788764613606590757)
XLA Ops:
  0.6 0.0 copy-start
  0.6 0.9 copy-done
  1.5 0.0 copy-start.1
  1.6 0.9 copy-done.1
  2.5 0.0 copy-start.2
  2.5 0.7 copy-done.2
  3.2 156.0 %shard_map.94 = (bf16[1,128,5120]{2,1,0:T(8,128)(2,1)}, f32[128,640]{1,0:T(8,128)S(1)}, f32[128,640]{1,0:T(8,128)S(1)}) custom-call(bf16[1,1,128,4096]{3,2,1,0:T(8,128)(2,1)} %enc.1, bf16[1,128,4096]{2,1,0:T(8,128)(2,1)} %resid.1, f32[1,4096]{1,0:T(1,128)S(1)} %bitcast.1, bf16[128,640]{1,0:T(8,128)(2,1)S(1)} %copy-done, bf16[128,640]{1,0:T(8,128)(2,1)S(1)} %copy-done.1, ...), custom_call_target="tpu_custom_call" | custom-call | flops 4000000000 | bytes 10000000 | tf_op jit(solution)/shard_map/pallas_call | solution.py:403
  159.2 2.5 %copy.13 = bf16[1,128,5120]{2,1,0:T(8,128)(2,1)} copy(bf16[1,128,5120]{2,1,0:T(8,128)(2,1)} %get-tuple-element.6) | data formatting | bytes 2621440
  161.7 0.7 copy.14
  162.4 0.7 copy.15
Async XLA Ops:
  0.6 0.9 copy-start
  1.5 0.9 copy-start.1
  2.5 0.7 copy-start.2

commit v2 on v0

v2 whole, which is shorter than its diff:
```python
import jax
import jax.numpy as jnp
from jax import lax
from jax.experimental import pallas as pl
from jax.experimental.pallas import tpu as pltpu
from jax.sharding import PartitionSpec as P

MESH = pl.DeviceIdType.MESH
HEAD = 128
F32 = jnp.float32
BF16 = jnp.bfloat16
CUTS = ((0, 256), (256, 640))


def dot(a, b, ca, cb):
    return lax.dot_general(a, b, (((ca,), (cb,)), ((), ())), preferred_element_type=F32)


def each(start, stop, body):
    lax.fori_loop(start, stop, lambda i, c: (body(i), c)[1], 0)


def device(x, z, k, l, y):
    return ((x * 4 + z) * 2 + k, l * 4 + y)


def kernel(
    enc, resid, gain, key_w, val_w, queries, grads,
    out_q, out_k, out_v,
    enc_buf, res_buf, ez_own, ez_recv, text32, text, text_t, w_own, w_all, kv_part, kv_recv, kv, q_buf, g_buf, qg_buf,
    pg_send, pg_own, pg_recv, gr_own, gr_all, dw_part, dw_recv,
    loc, e_s, e_r, ez_s, ez_r, t1_s, t1_r, t2_s, t2_r, t3_s, t3_r, w_s, w_r, kv_s, kv_r, kx_s, kx_r,
    qg_s, qg_r, px_s, px_r, oq_s, oq_r, ga_s, ga_r, dw_s, dw_r,
):
    clip, seq = lax.axis_index("clip"), lax.axis_index("seq")
    x, z, k = lax.div(clip, 8), lax.rem(lax.div(clip, 2), 4), lax.rem(clip, 2)
    l, y = lax.div(seq, 4), lax.rem(seq, 4)
    el, ek = 1 - l, 1 - k
    my_row, my_clip = z * 2 + k, k * 4 + x

    def y_dev(y2):
        return device(x, z, k, l, y2)

    def row_dev(e):
        return device(x, lax.div(e, 2), lax.rem(e, 2), l, y)

    def clip_dev(e):
        return device(lax.rem(e, 4), z, lax.div(e, 4), l, y)

    def others(n, me, body):
        each(1, n, lambda o: body(lax.rem(me + o, n)))

    def remote(src, dst, s, r, where):
        return pltpu.make_async_remote_copy(
            src_ref=src, dst_ref=dst, send_sem=s, recv_sem=r, device_id=where, device_id_type=MESH
        )

    def local(src, dst, i):
        return pltpu.make_async_copy(src, dst, loc.at[i])

    sends, arrivals = [], {}

    def arrive(name):
        for wait in arrivals.pop(name):
            wait()

    def flush():
        for name in list(arrivals):
            arrive(name)
        for wait in sends:
            wait()

    def group(name, n, me, copy):
        others(n, me, lambda e: copy(e, me).start())
        sends.append(lambda: others(n, me, lambda e: copy(e, me).wait_send()))
        arrivals[name] = [lambda: others(n, me, lambda e: copy(e, e).wait_recv())]

    def pair(name, copy, back):
        copy.start()
        sends.append(copy.wait_send)
        arrivals[name] = [back.wait_recv]

    def keep(name, copy):
        copy.start()
        arrivals.setdefault(name, []).append(copy.wait)

    def rows_of(i, n):
        return pl.ds(pl.multiple_of(i * n, n), n)

    def columns(j):
        return pl.ds(pl.multiple_of(j * 640, 128), 640)

    keep("enc", local(enc.at[0, 0, rows_of(y, 32)], enc_buf.at[y], 0))
    keep("resid", local(resid.at[0, rows_of(y, 32)], res_buf, 1))
    keep("w_own", local(key_w, w_own.at[0], 2))
    keep("w_own", local(val_w, w_own.at[1], 3))

    def qg_copy(i, l2, y2, slot):
        src, dst = ((queries, q_buf), (grads, g_buf))[i]
        return remote(
            src.at[0, :, columns(l2 * 4 + y2)], dst.at[l2, rows_of(slot, 128)],
            qg_s.at[i, l2, y2], qg_r.at[i, l2, slot], y_dev(y2),
        )

    def qg_own(i, l2):
        src, dst = ((queries, q_buf), (grads, g_buf))[i]
        return local(src.at[0, :, columns(l2 * 4 + y)], dst.at[l2, rows_of(y, 128)], 4 + 2 * i + l2)

    def qg_start(name, l2):
        group(name + "_q", 4, y, lambda y2, slot: qg_copy(0, l2, y2, slot))
        group(name + "_g", 4, y, lambda y2, slot: qg_copy(1, l2, y2, slot))

    for i in range(2):
        keep("mine", qg_own(i, 0))
        keep("mine", qg_own(i, 1))

    bar = pltpu.get_barrier_semaphore()

    def greet(where):
        pl.semaphore_signal(bar, inc=1, device_id=where, device_id_type=MESH)

    others(4, y, lambda e: greet(y_dev(e)))
    greet(device(x, z, k, el, y))
    others(8, my_row, lambda e: greet(row_dev(e)))
    others(8, my_clip, lambda e: greet(clip_dev(e)))
    pl.semaphore_wait(bar, 18)

    def enc_copy(y2, slot):
        return remote(
            enc.at[0, 0, rows_of(y2, 32)], enc_buf.at[slot], e_s.at[y2], e_r.at[slot], y_dev(y2)
        )

    group("enc_y", 4, y, enc_copy)

    arrive("w_own")

    def w_copy(e, slot):
        return remote(
            w_own.at[lax.rem(e, 2)], w_all.at[slot], w_s.at[e], w_r.at[slot], row_dev(e)
        )

    for o in (1, 3):
        for k2 in range(2):
            w_copy(lax.rem(z + o, 4) * 2 + k2, my_row).start()
    w_copy(z * 2 + ek, my_row).start()
    sends.append(lambda: others(8, my_row, lambda e: w_copy(e, my_row).wait_send()))
    arrivals["w"] = [lambda: others(8, my_row, lambda e: w_copy(e, e).wait_recv())]
    keep("w", local(w_own.at[k], w_all.at[my_row], 8))

    arrive("enc")
    arrive("resid")
    arrive("enc_y")
    for b in range(4):
        cols = pl.ds(b * 1024, 1024)
        part = enc_buf[0, :, cols].astype(F32)
        for s in range(1, 4):
            part = part + enc_buf[s, :, cols].astype(F32)
        ez_own[:, cols] = part.astype(BF16)
    ez = remote(ez_own, ez_recv, ez_s.at[0], ez_r.at[0], device(x, z, k, el, y))
    pair("ez", ez, ez)
    qg_start("own", l)
    arrive("ez")
    for k2 in range(2):
        w_copy(lax.rem(z + 2, 4) * 2 + k2, my_row).start()

    def hidden(b):
        cols = pl.ds(b * 1024, 1024)
        return (ez_own[:, cols].astype(F32) + ez_recv[:, cols].astype(F32)) + res_buf[:, cols].astype(F32)

    total = jnp.zeros((32, 1), F32)
    for b in range(4):
        h = hidden(b)
        total = total + jnp.sum(h * h, axis=1, keepdims=True)
    inv = lax.rsqrt(total * (1.0 / 4096.0) + 1e-06)
    for b in range(4):
        text32[b] = (hidden(b) * inv * gain[:, pl.ds(b * 1024, 1024)]).astype(BF16)

    def t1_copy(x2, slot):
        return remote(
            text32.at[x2], text.at[k, slot, rows_of(y, 32)], t1_s.at[x2], t1_r.at[slot], device(x2, z, k, l, y)
        )

    group("t1", 4, x, t1_copy)
    keep("t1", local(text32.at[x], text.at[k, x, rows_of(y, 32)], 9))
    arrive("t1")

    def t2_copy(y2, slot):
        part = text.at[k, :, rows_of(slot, 32)]
        return remote(part, part, t2_s.at[y2], t2_r.at[slot], y_dev(y2))

    group("t2", 4, y, t2_copy)
    arrive("t2")

    def t3_copy(core):
        return remote(text.at[core], text.at[core], t3_s.at[0], t3_r.at[0], device(x, z, ek, l, y))

    pair("t3", t3_copy(k), t3_copy(ek))
    qg_start("far", el)
    arrive("w")

    def kv_copy(c, e, slot):
        cols = pl.ds(CUTS[c][0], CUTS[c][1] - CUTS[c][0])
        return remote(
            kv_part.at[lax.div(e, 4), lax.rem(e, 4), :, cols],
            kv_recv.at[lax.div(slot, 4), lax.rem(slot, 4), :, cols],
            kv_s.at[c, e], kv_r.at[c, slot], clip_dev(e),
        )

    def project(core, c):
        lo, hi = CUTS[c]
        t = text[core].reshape(512, 1024)
        acc = dot(t, w_all[:, :, lo:hi].reshape(1024, hi - lo), 1, 0)
        kv_part[core, :, :, lo:hi] = acc.astype(BF16).reshape(4, 128, hi - lo)

    for c, (lo, hi) in enumerate(CUTS):
        cols = pl.ds(lo, hi - lo)
        project(k, c)
        others(4, x, lambda x2: kv_copy(c, k * 4 + x2, my_clip).start())
        keep(f"kv{c}", local(kv_part.at[k, x, :, cols], kv_recv.at[k, x, :, cols], 10 + c))
        if c == 0:
            arrive("t3")
        project(ek, c)
        each(0, 4, lambda o: kv_copy(c, ek * 4 + lax.rem(x + o, 4), my_clip).start())
        sends.append(lambda c=c: others(8, my_clip, lambda e: kv_copy(c, e, my_clip).wait_send()))
        arrivals[f"kv{c}"].append(lambda c=c: others(8, my_clip, lambda e: kv_copy(c, e, e).wait_recv()))

    def turn(z2):
        text_t[z2] = text[:, :, :, rows_of(z2, 256)].reshape(1024, 256).T

    each(0, 4, turn)

    def kx_copy(c, slot):
        part = kv.at[slot, :, :, pl.ds(CUTS[c][0], CUTS[c][1] - CUTS[c][0])]
        return remote(part, part, kx_s.at[c], kx_r.at[c], device(x, z, k, el, y))

    def gather_kv(c):
        lo, hi = CUTS[c]
        arrive(f"kv{c}")
        for i in range(2):
            acc = kv_recv[i, 0, :, lo:hi].astype(F32)
            for b in range(1, 4):
                acc = acc + kv_recv[i, b, :, lo:hi].astype(F32)
            kv[l, i, :, lo:hi] = acc.astype(BF16)
        pair(f"kx{c}", kx_copy(c, l), kx_copy(c, el))

    scale = HEAD ** (-0.5)

    def head(l2, c, keep):
        cols = pl.ds(pl.multiple_of(c * HEAD, HEAD), HEAD)
        qh, gh = q_buf[l2, :, cols], g_buf[l2, :, cols]
        kh, vh = kv[l2, 0, :, cols], kv[l2, 1, :, cols]
        e = jnp.exp(dot(kh, qh, 1, 1) * scale)
        probs = e * (1.0 / jnp.sum(e, axis=0, keepdims=True))
        probs_b = probs.astype(BF16)
        dprobs = dot(vh, gh, 1, 1)
        delta = jnp.sum(probs_b.astype(F32) * dprobs, axis=0, keepdims=True)
        ds = (probs * (dprobs - delta)).astype(BF16)
        qg_buf[l2, :, cols] = (dot(ds, kh, 0, 0) * scale).astype(BF16)
        keep[0, :, cols] = (dot(ds, qh, 1, 0) * scale).astype(keep.dtype)
        keep[1, :, cols] = dot(probs_b, gh, 1, 0).astype(keep.dtype)

    def heads(l2, c, keep):
        lo, hi = CUTS[c]
        each(lo // HEAD, hi // HEAD, lambda h: head(l2, h, keep))

    def px_start(c):
        lo, hi = CUTS[c]
        cols = pl.ds(lo, hi - lo)
        copy = remote(
            pg_send.at[:, :, cols], pg_recv.at[:, :, cols], px_s.at[c], px_r.at[c], device(x, z, k, el, y)
        )
        pair(f"px{c}", copy, copy)

    def oq_copy(l2, y2, slot):
        return remote(
            qg_buf.at[l2, rows_of(y2, 128)], out_q.at[0, :, columns(l2 * 4 + slot)],
            oq_s.at[l2, y2], oq_r.at[l2, slot], y_dev(y2),
        )

    def oq_start(name, l2, i):
        group(name, 4, y, lambda y2, slot: oq_copy(l2, y2, slot))
        keep(name, local(qg_buf.at[l2, rows_of(y, 128)], out_q.at[0, :, columns(l2 * 4 + y)], i))

    def ga_copy(c, e, slot):
        cols = pl.ds(CUTS[c][0], CUTS[c][1] - CUTS[c][0])
        return remote(
            gr_own.at[lax.div(e, 4), :, cols], gr_all.at[lax.div(slot, 4), lax.rem(slot, 4), :, cols],
            ga_s.at[c, e], ga_r.at[c, slot], clip_dev(e),
        )

    def ga_start(c):
        lo, hi = CUTS[c]
        cols = pl.ds(lo, hi - lo)
        arrive(f"px{c}")
        gr_own[:, :, lo:hi] = (pg_own[:, :, lo:hi] + pg_recv[:, :, lo:hi].astype(F32)).astype(BF16)
        group(f"ga{c}", 8, my_clip, lambda e, slot: ga_copy(c, e, slot))
        keep(f"ga{c}", local(gr_own.at[k, :, cols], gr_all.at[k, x, :, cols], 14 + c))

    def dw_copy(c, e, slot):
        cols = pl.ds(CUTS[c][0], CUTS[c][1] - CUTS[c][0])
        return remote(
            dw_part.at[e, :, cols], dw_recv.at[lax.rem(slot, 2), lax.div(slot, 2), :, cols],
            dw_s.at[c, e], dw_r.at[c, slot], row_dev(e),
        )

    def dw_start(c):
        lo, hi = CUTS[c]
        cols = pl.ds(lo, hi - lo)
        arrive(f"ga{c}")

        def step(z2):
            acc = dot(text_t[z2], gr_all[:, :, :, lo:hi].reshape(1024, hi - lo), 1, 0)
            dw_part[pl.ds(z2 * 2, 2), :, lo:hi] = acc.astype(BF16).reshape(2, 128, hi - lo)

        def step_send(z2):
            step(z2)
            for k2 in range(2):
                dw_copy(c, z2 * 2 + k2, my_row).start()

        others(4, z, step_send)
        step(z)
        dw_copy(c, z * 2 + ek, my_row).start()
        sends.append(lambda: others(8, my_row, lambda e: dw_copy(c, e, my_row).wait_send()))
        arrivals[f"dw{c}"] = [lambda: others(8, my_row, lambda e: dw_copy(c, e, e).wait_recv())]
        keep(f"dw{c}", local(dw_part.at[my_row, :, cols], dw_recv.at[k, z, :, cols], 16 + c))

    def dw_end(c):
        lo, hi = CUTS[c]
        arrive(f"dw{c}")
        for i, out in ((0, out_k), (1, out_v)):
            acc = dw_recv[i, 0, :, lo:hi].astype(F32)
            for b in range(1, 4):
                acc = acc + dw_recv[i, b, :, lo:hi].astype(F32)
            out[:, lo:hi] = acc

    gather_kv(0)
    arrive("mine")
    for i in "qg":
        arrive("own_" + i)
    heads(l, 0, pg_own)
    gather_kv(1)
    for i in "qg":
        arrive("far_" + i)
    arrive("kx0")
    heads(el, 0, pg_send)
    px_start(0)
    heads(l, 1, pg_own)
    oq_start("oq_own", l, 12)
    ga_start(0)
    arrive("kx1")
    heads(el, 1, pg_send)
    px_start(1)
    oq_start("oq_far", el, 13)
    dw_start(0)
    ga_start(1)
    dw_start(1)
    dw_end(0)
    dw_end(1)
    flush()


def on_device(enc_terms, enc_resid, norm_gain, key_weight, value_weight, queries, out_grad):
    any_spec = pl.BlockSpec(memory_space=pl.ANY)
    vmem = pl.BlockSpec(memory_space=pltpu.VMEM)
    dma = pltpu.SemaphoreType.DMA
    scratch = [
        pltpu.VMEM((4, 32, 4096), BF16),
        pltpu.VMEM((32, 4096), BF16),
        pltpu.VMEM((32, 4096), BF16),
        pltpu.VMEM((32, 4096), BF16),
        pltpu.VMEM((4, 32, 1024), BF16),
        pltpu.VMEM((2, 4, 128, 1024), BF16),
        pltpu.VMEM((4, 256, 1024), BF16),
        pltpu.VMEM((2, 128, 640), BF16),
        pltpu.VMEM((8, 128, 640), BF16),
        pltpu.VMEM((2, 4, 128, 640), BF16),
        pltpu.VMEM((2, 4, 128, 640), BF16),
        pltpu.VMEM((2, 2, 128, 640), BF16),
        pltpu.VMEM((2, 512, 640), BF16),
        pltpu.VMEM((2, 512, 640), BF16),
        pltpu.VMEM((2, 512, 640), BF16),
        pltpu.VMEM((2, 128, 640), BF16),
        pltpu.VMEM((2, 128, 640), F32),
        pltpu.VMEM((2, 128, 640), BF16),
        pltpu.VMEM((2, 128, 640), BF16),
        pltpu.VMEM((2, 4, 128, 640), BF16),
        pltpu.VMEM((8, 128, 640), BF16),
        pltpu.VMEM((2, 4, 128, 640), BF16),
        dma((18,)),
        dma((4,)), dma((4,)),
        dma((1,)), dma((1,)),
        dma((4,)), dma((4,)),
        dma((4,)), dma((4,)),
        dma((1,)), dma((1,)),
        dma((8,)), dma((8,)),
        dma((2, 8)), dma((2, 8)),
        dma((2,)), dma((2,)),
        dma((2, 2, 4)), dma((2, 2, 4)),
        dma((2,)), dma((2,)),
        dma((2, 4)), dma((2, 4)),
        dma((2, 8)), dma((2, 8)),
        dma((2, 8)), dma((2, 8)),
    ]
    return pl.pallas_call(
        kernel,
        out_shape=(
            jax.ShapeDtypeStruct(queries.shape, BF16),
            jax.ShapeDtypeStruct(key_weight.shape, F32),
            jax.ShapeDtypeStruct(value_weight.shape, F32),
        ),
        in_specs=[any_spec, any_spec, vmem, any_spec, any_spec, any_spec, any_spec],
        out_specs=(any_spec, vmem, vmem),
        scratch_shapes=scratch,
        compiler_params=pltpu.CompilerParams(
            collective_id=0, has_side_effects=True, vmem_limit_bytes=52 * 2**20
        ),
        cost_estimate=pl.CostEstimate(flops=4 * 10**9, bytes_accessed=10**7, transcendentals=655360),
    )(enc_terms, enc_resid, norm_gain.reshape(1, -1), key_weight, value_weight, queries, out_grad)


def solution(mesh):
    in_specs = (
        P("clip", "seq", None, None),
        P("clip", None, None),
        P(),
        P("clip", "seq"),
        P("clip", "seq"),
        P("clip", "seq", None),
        P("clip", "seq", None),
    )
    out_specs = (P("clip", "seq", None), P("clip", "seq"), P("clip", "seq"))
    return jax.shard_map(
        on_device, mesh=mesh, in_specs=in_specs, out_specs=out_specs, check_vma=False
    )
```

time: 479 us -> 128 us (0.27)
  waiting for transfers between devices: 411 us -> 0 us
  Pallas kernels: 0 us -> 120 us
  matrix products: 32.2 us -> 0 us
  between operations: 15.6 us -> 0.65 us
  local copies, waits for them, and re-layouts: 16.4 us -> 6.45 us
    reduce_scatter x3 -> x0, waiting for transfers between devices: 211 us -> none  [the longest x1 129 us: on_device(): lax.psum_scatter(lax.dot_general(columns, both_grads, (((0,), (0,)), ((),...]
    pallas_call x0 -> x1, Pallas kernels: none -> 120 us  [on_device(): pl.pallas_call(kernel, out_shape=(jax.ShapeDtypeStruct(queries.shape, BF1...]
    all_gather x4 -> x0, waiting for transfers between devices: 111 us -> none  [the longest x1 43.5 us: on_device(): lax.all_gather(value_weight, 'clip', axis=0, tiled=True)]
    psum x1 -> x0, waiting for transfers between devices: 88.4 us -> none  [on_device(): lax.psum(partial_terms.astype(jnp.bfloat16), 'seq').astype(jnp.float32)]
    dot_general x9 -> x0, matrix products: 32.2 us -> none  [the longest x1 6.55 us: on_device(): lax.dot_general(columns, both_grads, (((0,), (0,)), ((), ())), preferred_...]
  transfers between devices with their start and end apart: 8 -> 0, of which waited for: 7 -> 0; matrix products, arithmetic and copies ran while one was open for 6% -> 0% of each run, Pallas kernels for 0% -> 0%
where the time goes in v2:
time: 128 us; the launch traced here: 127 us
  Pallas kernels  120 us (94%)
  local copies, waits for them, and re-layouts  6.45 us (5%)
    pallas_call x1, Pallas kernels, on_device(): pl.pallas_call(kernel, out_shape=(jax.ShapeDtypeStruct(queries.shape, BF1...  120 us
    unnamed x9, local copies, waits for them, and re-layouts  6.45 us

profile of v2, /device:TPU:1, one launch (start us, length us, event | category | flops | bytes accessed | tf_op | source)
XLA Modules:
  0.0 127.2 jit_solution(9495156900317895090)
XLA Ops:
  0.6 0.0 copy-start
  0.6 0.9 copy-done
  1.5 0.0 copy-start.1
  1.6 0.9 copy-done.1
  2.5 0.0 copy-start.2
  2.5 0.7 copy-done.2
  3.2 120.1 %shard_map.94 = (bf16[1,128,5120]{2,1,0:T(8,128)(2,1)}, f32[128,640]{1,0:T(8,128)S(1)}, f32[128,640]{1,0:T(8,128)S(1)}) custom-call(bf16[1,1,128,4096]{3,2,1,0:T(8,128)(2,1)} %enc.1, bf16[1,128,4096]{2,1,0:T(8,128)(2,1)} %resid.1, f32[1,4096]{1,0:T(1,128)S(1)} %bitcast.1, bf16[128,640]{1,0:T(8,128)(2,1)S(1)} %copy-done, bf16[128,640]{1,0:T(8,128)(2,1)S(1)} %copy-done.1, ...), custom_call_target="tpu_custom_call" | custom-call | flops 4000000000 | bytes 10000000 | tf_op jit(solution)/shard_map/pallas_call | solution.py:404
  123.3 2.5 %copy.13 = bf16[1,128,5120]{2,1,0:T(8,128)(2,1)} copy(bf16[1,128,5120]{2,1,0:T(8,128)(2,1)} %get-tuple-element.6) | data formatting | bytes 2621440
  125.8 0.7 copy.14
  126.5 0.7 copy.15
Async XLA Ops:
  0.6 0.9 copy-start
  1.5 0.9 copy-start.1
  2.5 0.7 copy-start.2

commit v3 on v2

--- a/solution.py
+++ b/solution.py
@@ -9,7 +9,7 @@
 HEAD = 128
 F32 = jnp.float32
 BF16 = jnp.bfloat16
-CUTS = ((0, 256), (256, 640))
+CUTS = ((0, 128), (128, 384), (384, 640))
 
 
 def dot(a, b, ca, cb):
@@ -28,9 +28,9 @@
     enc, resid, gain, key_w, val_w, queries, grads,
     out_q, out_k, out_v,
     enc_buf, res_buf, ez_own, ez_recv, text32, text, text_t, w_own, w_all, kv_part, kv_recv, kv, q_buf, g_buf, qg_buf,
-    pg_send, pg_own, pg_recv, gr_own, gr_all, dw_part, dw_recv,
-    loc, e_s, e_r, ez_s, ez_r, t1_s, t1_r, t2_s, t2_r, t3_s, t3_r, w_s, w_r, kv_s, kv_r, kx_s, kx_r,
-    qg_s, qg_r, px_s, px_r, oq_s, oq_r, ga_s, ga_r, dw_s, dw_r,
+    pg_send, pg_own, pg_recv, gr_own, gr_all, dw_part, dw_recv, dw_mid,
+    loc, e_s, e_r, ez_s, ez_r, t1_s, t1_r, t2_s, t2_r, t3_s, t3_r, w_s, w_r, wf_s, wf_r, kv_s, kv_r, kx_s, kx_r,
+    qg_s, qg_r, px_s, px_r, oq_s, oq_r, ga_s, ga_r, dw_s, dw_r, dp_s, dp_r,
 ):
     clip, seq = lax.axis_index("clip"), lax.axis_index("seq")
     x, z, k = lax.div(clip, 8), lax.rem(lax.div(clip, 2), 4), lax.rem(clip, 2)
@@ -95,20 +95,22 @@
     keep("w_own", local(key_w, w_own.at[0], 2))
     keep("w_own", local(val_w, w_own.at[1], 3))
 
-    def qg_copy(i, l2, y2, slot):
+    def qg_copy(i, l2, c, y2, slot):
         src, dst = ((queries, q_buf), (grads, g_buf))[i]
-        return remote(
-            src.at[0, :, columns(l2 * 4 + y2)], dst.at[l2, rows_of(slot, 128)],
-            qg_s.at[i, l2, y2], qg_r.at[i, l2, slot], y_dev(y2),
+        lo, hi = CUTS[c]
+        return remote(
+            src.at[0, :, pl.ds(pl.multiple_of((l2 * 4 + y2) * 640 + lo, 128), hi - lo)],
+            dst.at[l2, rows_of(slot, 128), pl.ds(lo, hi - lo)],
+            qg_s.at[i, l2, c, y2], qg_r.at[i, l2, c, slot], y_dev(y2),
         )
 
     def qg_own(i, l2):
         src, dst = ((queries, q_buf), (grads, g_buf))[i]
         return local(src.at[0, :, columns(l2 * 4 + y)], dst.at[l2, rows_of(y, 128)], 4 + 2 * i + l2)
 
-    def qg_start(name, l2):
-        group(name + "_q", 4, y, lambda y2, slot: qg_copy(0, l2, y2, slot))
-        group(name + "_g", 4, y, lambda y2, slot: qg_copy(1, l2, y2, slot))
+    def qg_start(name, l2, c):
+        for i in range(2):
+            group(f"{name}_{c}_{i}", 4, y, lambda y2, slot, i=i: qg_copy(i, l2, c, y2, slot))
 
     for i in range(2):
         keep("mine", qg_own(i, 0))
@@ -121,47 +123,63 @@
 
     others(4, y, lambda e: greet(y_dev(e)))
     greet(device(x, z, k, el, y))
-    others(8, my_row, lambda e: greet(row_dev(e)))
-    others(8, my_clip, lambda e: greet(clip_dev(e)))
-    pl.semaphore_wait(bar, 18)
-
-    def enc_copy(y2, slot):
-        return remote(
-            enc.at[0, 0, rows_of(y2, 32)], enc_buf.at[slot], e_s.at[y2], e_r.at[slot], y_dev(y2)
-        )
-
-    group("enc_y", 4, y, enc_copy)
-
-    arrive("w_own")
-
-    def w_copy(e, slot):
-        return remote(
-            w_own.at[lax.rem(e, 2)], w_all.at[slot], w_s.at[e], w_r.at[slot], row_dev(e)
-        )
-
     for o in (1, 3):
         for k2 in range(2):
-            w_copy(lax.rem(z + o, 4) * 2 + k2, my_row).start()
-    w_copy(z * 2 + ek, my_row).start()
-    sends.append(lambda: others(8, my_row, lambda e: w_copy(e, my_row).wait_send()))
-    arrivals["w"] = [lambda: others(8, my_row, lambda e: w_copy(e, e).wait_recv())]
+            greet(device(x, lax.rem(z + o, 4), k2, l, y))
+    greet(device(x, z, ek, l, y))
+    others(8, my_clip, lambda e: greet(clip_dev(e)))
+    pl.semaphore_wait(bar, 16)
+
+    def enc_copy(h, y2, slot):
+        cols = pl.ds(h * 2048, 2048)
+        return remote(
+            enc.at[0, 0, rows_of(y2, 32), cols], enc_buf.at[slot, :, cols], e_s.at[h, y2], e_r.at[h, slot], y_dev(y2)
+        )
+
+    group("enc_0", 4, y, lambda y2, slot: enc_copy(0, y2, slot))
+    group("enc_1", 4, y, lambda y2, slot: enc_copy(1, y2, slot))
+
+    arrive("w_own")
+
+    def w_copy(e, slot):
+        return remote(
+            w_own.at[lax.rem(e, 2)], w_all.at[slot], w_s.at[e], w_r.at[slot], row_dev(e)
+        )
+
+    near = [(o, k2) for o in (1, 3) for k2 in range(2)]
+
+    def near_row(o, k2):
+        return lax.rem(z + o, 4) * 2 + k2
+
+    def w_start(e):
+        w_copy(e, my_row).start()
+        sends.append(lambda: w_copy(e, my_row).wait_send())
+
+    for o, k2 in near:
+        w_start(near_row(o, k2))
+    w_start(z * 2 + ek)
+    arrivals["w_near"] = [lambda e=near_row(o, k2): w_copy(e, e).wait_recv() for o, k2 in near]
+    arrivals["w"] = [lambda: w_copy(z * 2 + ek, z * 2 + ek).wait_recv()]
     keep("w", local(w_own.at[k], w_all.at[my_row], 8))
 
     arrive("enc")
     arrive("resid")
-    arrive("enc_y")
-    for b in range(4):
-        cols = pl.ds(b * 1024, 1024)
-        part = enc_buf[0, :, cols].astype(F32)
-        for s in range(1, 4):
-            part = part + enc_buf[s, :, cols].astype(F32)
-        ez_own[:, cols] = part.astype(BF16)
-    ez = remote(ez_own, ez_recv, ez_s.at[0], ez_r.at[0], device(x, z, k, el, y))
-    pair("ez", ez, ez)
-    qg_start("own", l)
-    arrive("ez")
-    for k2 in range(2):
-        w_copy(lax.rem(z + 2, 4) * 2 + k2, my_row).start()
+    for h in range(2):
+        arrive(f"enc_{h}")
+        for b in (2 * h, 2 * h + 1):
+            cols = pl.ds(b * 1024, 1024)
+            part = enc_buf[0, :, cols].astype(F32)
+            for i in range(1, 4):
+                part = part + enc_buf[i, :, cols].astype(F32)
+            ez_own[:, cols] = part.astype(BF16)
+        cols = pl.ds(h * 2048, 2048)
+        ez = remote(ez_own.at[:, cols], ez_recv.at[:, cols], ez_s.at[h], ez_r.at[h], device(x, z, k, el, y))
+        pair(f"ez_{h}", ez, ez)
+    qg_start("own", l, 0)
+    qg_start("far", el, 0)
+    qg_start("own", l, 1)
+    arrive("ez_0")
+    arrive("ez_1")
 
     def hidden(b):
         cols = pl.ds(b * 1024, 1024)
@@ -181,48 +199,76 @@
         )
 
     group("t1", 4, x, t1_copy)
+    arrivals.pop("t1")
     keep("t1", local(text32.at[x], text.at[k, x, rows_of(y, 32)], 9))
-    arrive("t1")
-
-    def t2_copy(y2, slot):
-        part = text.at[k, :, rows_of(slot, 32)]
-        return remote(part, part, t2_s.at[y2], t2_r.at[slot], y_dev(y2))
-
-    group("t2", 4, y, t2_copy)
-    arrive("t2")
-
-    def t3_copy(core):
-        return remote(text.at[core], text.at[core], t3_s.at[0], t3_r.at[0], device(x, z, ek, l, y))
-
-    pair("t3", t3_copy(k), t3_copy(ek))
-    qg_start("far", el)
-    arrive("w")
-
-    def kv_copy(c, e, slot):
-        cols = pl.ds(CUTS[c][0], CUTS[c][1] - CUTS[c][0])
-        return remote(
-            kv_part.at[lax.div(e, 4), lax.rem(e, 4), :, cols],
-            kv_recv.at[lax.div(slot, 4), lax.rem(slot, 4), :, cols],
-            kv_s.at[c, e], kv_r.at[c, slot], clip_dev(e),
-        )
-
-    def project(core, c):
-        lo, hi = CUTS[c]
-        t = text[core].reshape(512, 1024)
-        acc = dot(t, w_all[:, :, lo:hi].reshape(1024, hi - lo), 1, 0)
-        kv_part[core, :, :, lo:hi] = acc.astype(BF16).reshape(4, 128, hi - lo)
-
-    for c, (lo, hi) in enumerate(CUTS):
-        cols = pl.ds(lo, hi - lo)
-        project(k, c)
-        others(4, x, lambda x2: kv_copy(c, k * 4 + x2, my_clip).start())
-        keep(f"kv{c}", local(kv_part.at[k, x, :, cols], kv_recv.at[k, x, :, cols], 10 + c))
-        if c == 0:
-            arrive("t3")
-        project(ek, c)
-        each(0, 4, lambda o: kv_copy(c, ek * 4 + lax.rem(x + o, 4), my_clip).start())
-        sends.append(lambda c=c: others(8, my_clip, lambda e: kv_copy(c, e, my_clip).wait_send()))
-        arrivals[f"kv{c}"].append(lambda c=c: others(8, my_clip, lambda e: kv_copy(c, e, e).wait_recv()))
+
+    arrive("w_near")
+
+    def w_pass(i):
+        o = (3, 1)[i]
+        part = w_all.at[pl.ds(lax.rem(z + o, 4) * 2, 2), pl.ds(64 * i, 64)]
+        return remote(part, part, wf_s.at[i], wf_r.at[i], device(x, lax.rem(z + 4 - o, 4), k, l, y))
+
+    def w_passed(i):
+        part = w_all.at[pl.ds(lax.rem(z + 2, 4) * 2, 2), pl.ds(64 * i, 64)]
+        return remote(part, part, wf_s.at[i], wf_r.at[i], device(x, lax.rem(z + 1, 4), k, l, y))
+
+    for i in range(2):
+        pair(f"w_far{i}", w_pass(i), w_passed(i))
+
+    def t2_copy(x2, y2, slot):
+        part = text.at[k, x2, rows_of(slot, 32)]
+        return remote(part, part, t2_s.at[x2, y2], t2_r.at[x2, slot], y_dev(y2))
+
+    order = (0, 2, 1, 3)
+    for o in order:
+        x2 = lax.rem(x + o, 4)
+        if o == 0:
+            arrive("t1")
+        else:
+            t1_copy(x2, x2).wait_recv()
+        group(f"t2_{o}", 4, y, lambda y2, slot, x2=x2: t2_copy(x2, y2, slot))
+    qg_start("far", el, 1)
+    qg_start("own", l, 2)
+    qg_start("far", el, 2)
+
+    def t3_copy(core, x2):
+        part = text.at[core, x2]
+        return remote(part, part, t3_s.at[x2], t3_r.at[x2], device(x, z, ek, l, y))
+
+    def kv_copy(e, slot):
+        return remote(
+            kv_part.at[lax.div(e, 4), lax.rem(e, 4)], kv_recv.at[lax.div(slot, 4), lax.rem(slot, 4)],
+            kv_s.at[e], kv_r.at[slot], clip_dev(e),
+        )
+
+    def project(x2):
+        t = text[:, x2].reshape(256, 1024)
+        for lo, hi in ((0, 256), (256, 640)):
+            acc = dot(t, w_all[:, :, lo:hi].reshape(1024, hi - lo), 1, 0)
+            kv_part[:, x2, :, lo:hi] = acc.astype(BF16).reshape(2, 128, hi - lo)
+
+    def kv_start(core, x2):
+        e = core * 4 + x2
+        kv_copy(e, my_clip).start()
+        sends.append(lambda: kv_copy(e, my_clip).wait_send())
+
+    for o in order:
+        x2 = lax.rem(x + o, 4)
+        arrive(f"t2_{o}")
+        pair(f"t3_{o}", t3_copy(k, x2), t3_copy(ek, x2))
+        if o == 0:
+            arrive("w")
+            arrive("w_far0")
+            arrive("w_far1")
+        arrive(f"t3_{o}")
+        project(x2)
+        if o == 0:
+            keep("kv", local(kv_part.at[k, x], kv_recv.at[k, x], 10))
+        else:
+            kv_start(k, x2)
+        kv_start(ek, x2)
+    arrivals["kv"].append(lambda: others(8, my_clip, lambda e: kv_copy(e, e).wait_recv()))
 
     def turn(z2):
         text_t[z2] = text[:, :, :, rows_of(z2, 256)].reshape(1024, 256).T
@@ -235,7 +281,6 @@
 
     def gather_kv(c):
         lo, hi = CUTS[c]
-        arrive(f"kv{c}")
         for i in range(2):
             acc = kv_recv[i, 0, :, lo:hi].astype(F32)
             for b in range(1, 4):
@@ -294,7 +339,7 @@
         arrive(f"px{c}")
         gr_own[:, :, lo:hi] = (pg_own[:, :, lo:hi] + pg_recv[:, :, lo:hi].astype(F32)).astype(BF16)
         group(f"ga{c}", 8, my_clip, lambda e, slot: ga_copy(c, e, slot))
-        keep(f"ga{c}", local(gr_own.at[k, :, cols], gr_all.at[k, x, :, cols], 14 + c))
+        keep(f"ga{c}", local(gr_own.at[k, :, cols], gr_all.at[k, x, :, cols], 19 + c))
 
     def dw_copy(c, e, slot):
         cols = pl.ds(CUTS[c][0], CUTS[c][1] - CUTS[c][0])
@@ -303,59 +348,93 @@
             dw_s.at[c, e], dw_r.at[c, slot], row_dev(e),
         )
 
+    def dw_send(c, e):
+        dw_copy(c, e, my_row).start()
+        sends.append(lambda: dw_copy(c, e, my_row).wait_send())
+
+    def dw_pass(c, i):
+        cols = pl.ds(CUTS[c][0], CUTS[c][1] - CUTS[c][0])
+        return remote(
+            dw_part.at[lax.rem(z + 2, 4) * 2 + i, :, cols], dw_mid.at[i, :, cols],
+            dp_s.at[c, i], dp_r.at[c, i], device(x, lax.rem(z + (1, 3)[i], 4), k, l, y),
+        )
+
     def dw_start(c):
         lo, hi = CUTS[c]
         cols = pl.ds(lo, hi - lo)
         arrive(f"ga{c}")
+        grads_c = gr_all[:, :, :, lo:hi].reshape(1024, hi - lo)
 
         def step(z2):
-            acc = dot(text_t[z2], gr_all[:, :, :, lo:hi].reshape(1024, hi - lo), 1, 0)
+            acc = dot(text_t[z2], grads_c, 1, 0)
             dw_part[pl.ds(z2 * 2, 2), :, lo:hi] = acc.astype(BF16).reshape(2, 128, hi - lo)
 
-        def step_send(z2):
-            step(z2)
-            for k2 in range(2):
-                dw_copy(c, z2 * 2 + k2, my_row).start()
-
-        others(4, z, step_send)
+        step(lax.rem(z + 2, 4))
+        for i in range(2):
+            pair(f"dp{c}{i}", dw_pass(c, i), dw_pass(c, i))
+        for i, o in ((0, 1), (1, 3)):
+            step(lax.rem(z + o, 4))
+            dw_send(c, near_row(o, 1 - i))
         step(z)
-        dw_copy(c, z * 2 + ek, my_row).start()
-        sends.append(lambda: others(8, my_row, lambda e: dw_copy(c, e, my_row).wait_send()))
-        arrivals[f"dw{c}"] = [lambda: others(8, my_row, lambda e: dw_copy(c, e, e).wait_recv())]
-        keep(f"dw{c}", local(dw_part.at[my_row, :, cols], dw_recv.at[k, z, :, cols], 16 + c))
+        dw_send(c, z * 2 + ek)
+        keep(f"dw{c}", local(dw_part.at[my_row, :, cols], dw_recv.at[k, z, :, cols], 22 + c))
+        arrivals[f"dw{c}"] += [
+            lambda e=e: dw_copy(c, e, e).wait_recv()
+            for e in [near_row(o, k2) for o, k2 in near] + [z * 2 + ek]
+        ]
+
+    def dw_add(c):
+        lo, hi = CUTS[c]
+        for i, o in ((0, 1), (1, 3)):
+            arrive(f"dp{c}{i}")
+            e = near_row(o, i)
+            both = dw_part[e, :, lo:hi].astype(F32) + dw_mid[i, :, lo:hi].astype(F32)
+            dw_part[e, :, lo:hi] = both.astype(BF16)
+            dw_send(c, e)
 
     def dw_end(c):
         lo, hi = CUTS[c]
         arrive(f"dw{c}")
         for i, out in ((0, out_k), (1, out_v)):
-            acc = dw_recv[i, 0, :, lo:hi].astype(F32)
-            for b in range(1, 4):
-                acc = acc + dw_recv[i, b, :, lo:hi].astype(F32)
+            acc = dw_recv[i, z, :, lo:hi].astype(F32)
+            for o in (1, 3):
+                acc = acc + dw_recv[i, lax.rem(z + o, 4), :, lo:hi].astype(F32)
             out[:, lo:hi] = acc
 
+    last = len(CUTS) - 1
+    arrive("kv")
     gather_kv(0)
     arrive("mine")
-    for i in "qg":
-        arrive("own_" + i)
-    heads(l, 0, pg_own)
-    gather_kv(1)
-    for i in "qg":
-        arrive("far_" + i)
-    arrive("kx0")
-    heads(el, 0, pg_send)
-    px_start(0)
-    heads(l, 1, pg_own)
-    oq_start("oq_own", l, 12)
-    ga_start(0)
-    arrive("kx1")
-    heads(el, 1, pg_send)
-    px_start(1)
-    oq_start("oq_far", el, 13)
-    dw_start(0)
-    ga_start(1)
-    dw_start(1)
-    dw_end(0)
-    dw_end(1)
+
+    def heads_of(name, l2, c, kept):
+        for i in range(2):
+            arrive(f"{name}_{c}_{i}")
+        heads(l2, c, kept)
+
+    heads_of("own", l, 0, pg_own)
+    for c in range(len(CUTS)):
+        if c < last:
+            gather_kv(c + 1)
+        if c == 0:
+            pass
+        arrive(f"kx{c}")
+        heads_of("far", el, c, pg_send)
+        px_start(c)
+        if c < last:
+            heads_of("own", l, c + 1, pg_own)
+        if c == max(0, last - 1):
+            oq_start("oq_own", l, 12)
+        if c == last:
+            oq_start("oq_far", el, 13)
+        if c > 0:
+            dw_start(c - 1)
+        ga_start(c)
+        if c > 0:
+            dw_add(c - 1)
+    dw_start(last)
+    dw_add(last)
+    for c in range(len(CUTS)):
+        dw_end(c)
     flush()
 
 
@@ -386,20 +465,23 @@
         pltpu.VMEM((2, 4, 128, 640), BF16),
         pltpu.VMEM((8, 128, 640), BF16),
         pltpu.VMEM((2, 4, 128, 640), BF16),
-        dma((18,)),
+        pltpu.VMEM((2, 128, 640), BF16),
+        dma((25,)),
+        dma((2, 4)), dma((2, 4)),
+        dma((2,)), dma((2,)),
         dma((4,)), dma((4,)),
-        dma((1,)), dma((1,)),
+        dma((4, 4)), dma((4, 4)),
         dma((4,)), dma((4,)),
-        dma((4,)), dma((4,)),
-        dma((1,)), dma((1,)),
         dma((8,)), dma((8,)),
-        dma((2, 8)), dma((2, 8)),
         dma((2,)), dma((2,)),
-        dma((2, 2, 4)), dma((2, 2, 4)),
-        dma((2,)), dma((2,)),
+        dma((8,)), dma((8,)),
+        dma((3,)), dma((3,)),
+        dma((2, 2, 3, 4)), dma((2, 2, 3, 4)),
+        dma((3,)), dma((3,)),
         dma((2, 4)), dma((2, 4)),
-        dma((2, 8)), dma((2, 8)),
-        dma((2, 8)), dma((2, 8)),
+        dma((3, 8)), dma((3, 8)),
+        dma((3, 8)), dma((3, 8)),
+        dma((3, 2)), dma((3, 2)),
     ]
     return pl.pallas_call(
         kernel,
@@ -412,7 +494,7 @@
         out_specs=(any_spec, vmem, vmem),
         scratch_shapes=scratch,
         compiler_params=pltpu.CompilerParams(
-            collective_id=0, has_side_effects=True, vmem_limit_bytes=52 * 2**20
+            collective_id=0, has_side_effects=True, vmem_limit_bytes=62 * 2**20
         ),
         cost_estimate=pl.CostEstimate(flops=4 * 10**9, bytes_accessed=10**7, transcendentals=655360),
     )(enc_terms, enc_resid, norm_gain.reshape(1, -1), key_weight, value_weight, queries, out_grad)

time: 128 us -> 117 us (0.914)
  Pallas kernels: 120 us -> 112 us
  local copies, waits for them, and re-layouts: 6.45 us -> 3.98 us
    pallas_call x1, Pallas kernels: 120 us -> 112 us  [on_device(): pl.pallas_call(kernel, out_shape=(jax.ShapeDtypeStruct(queries.shape, BF1...]
    unnamed x9 -> x7, local copies, waits for them, and re-layouts: 6.45 us -> 3.98 us
where the time goes in v3:
time: 117 us
  Pallas kernels  112 us (96%)
  local copies, waits for them, and re-layouts  3.98 us (3%)
    pallas_call x1, Pallas kernels, on_device(): pl.pallas_call(kernel, out_shape=(jax.ShapeDtypeStruct(queries.shape, BF1...  112 us
    unnamed x7, local copies, waits for them, and re-layouts  3.98 us

profile of v3, /device:TPU:1, one launch (start us, length us, event | category | flops | bytes accessed | tf_op | source)
XLA Modules:
  0.0 116.6 jit_solution(555261047838337838)
XLA Ops:
  0.6 112.0 %shard_map.94 = (bf16[1,128,5120]{2,1,0:T(8,128)(2,1)}, f32[128,640]{1,0:T(8,128)}, f32[128,640]{1,0:T(8,128)}) custom-call(bf16[1,1,128,4096]{3,2,1,0:T(8,128)(2,1)} %enc.1, bf16[1,128,4096]{2,1,0:T(8,128)(2,1)} %resid.1, f32[1,4096]{1,0:T(1,128)} %bitcast.1, bf16[128,640]{1,0:T(8,128)(2,1)} %key_w.1, bf16[128,640]{1,0:T(8,128)(2,1)} %val_w.1, ...), custom_call_target="tpu_custom_call" | custom-call | flops 4000000000 | bytes 10000000 | tf_op jit(solution)/shard_map/pallas_call | solution.py:486
  112.6 0.0 copy-start.1
  112.6 0.0 copy-start
  112.6 2.5 %copy.13 = bf16[1,128,5120]{2,1,0:T(8,128)(2,1)} copy(bf16[1,128,5120]{2,1,0:T(8,128)(2,1)} %get-tuple-element.6) | data formatting | bytes 2621440
  115.2 0.0 copy-done.1
  115.2 0.7 copy.14
  115.9 0.0 copy-done
  115.9 0.7 copy.15
Async XLA Ops:
  112.6 2.5 %copy-start.1 = (f32[128,640]{1,0:T(8,128)S(1)}, f32[128,640]{1,0:T(8,128)}, u32[]{:S(2)}) copy-start(f32[128,640]{1,0:T(8,128)} %get-tuple-element.7) | copy-start | bytes 983044
  112.6 3.3 %copy-start = (f32[128,640]{1,0:T(8,128)S(1)}, f32[128,640]{1,0:T(8,128)}, u32[]{:S(2)}) copy-start(f32[128,640]{1,0:T(8,128)} %get-tuple-element.8) | copy-start | bytes 983044

commit v4 on v3

--- a/solution.py
+++ b/solution.py
@@ -10,6 +10,8 @@
 F32 = jnp.float32
 BF16 = jnp.bfloat16
 CUTS = ((0, 128), (128, 384), (384, 640))
+EARLY = 2
+HOLD = 0
 
 
 def dot(a, b, ca, cb):
@@ -112,6 +114,8 @@
         for i in range(2):
             group(f"{name}_{c}_{i}", 4, y, lambda y2, slot, i=i: qg_copy(i, l2, c, y2, slot))
 
+    pieces = [p for c in range(len(CUTS)) for p in (("own", l, c), ("far", el, c))]
+    early, late = pieces[:EARLY], pieces[EARLY:]
     for i in range(2):
         keep("mine", qg_own(i, 0))
         keep("mine", qg_own(i, 1))
@@ -175,9 +179,8 @@
         cols = pl.ds(h * 2048, 2048)
         ez = remote(ez_own.at[:, cols], ez_recv.at[:, cols], ez_s.at[h], ez_r.at[h], device(x, z, k, el, y))
         pair(f"ez_{h}", ez, ez)
-    qg_start("own", l, 0)
-    qg_start("far", el, 0)
-    qg_start("own", l, 1)
+    for name, l2, c in early:
+        qg_start(name, l2, c)
     arrive("ez_0")
     arrive("ez_1")
 
@@ -228,18 +231,19 @@
         else:
             t1_copy(x2, x2).wait_recv()
         group(f"t2_{o}", 4, y, lambda y2, slot, x2=x2: t2_copy(x2, y2, slot))
-    qg_start("far", el, 1)
-    qg_start("own", l, 2)
-    qg_start("far", el, 2)
+    for name, l2, c in late:
+        qg_start(name, l2, c)
 
     def t3_copy(core, x2):
         part = text.at[core, x2]
         return remote(part, part, t3_s.at[x2], t3_r.at[x2], device(x, z, ek, l, y))
 
-    def kv_copy(e, slot):
-        return remote(
-            kv_part.at[lax.div(e, 4), lax.rem(e, 4)], kv_recv.at[lax.div(slot, 4), lax.rem(slot, 4)],
-            kv_s.at[e], kv_r.at[slot], clip_dev(e),
+    def kv_copy(c, e, slot):
+        cols = pl.ds(CUTS[c][0], CUTS[c][1] - CUTS[c][0])
+        return remote(
+            kv_part.at[lax.div(e, 4), lax.rem(e, 4), :, cols],
+            kv_recv.at[lax.div(slot, 4), lax.rem(slot, 4), :, cols],
+            kv_s.at[c, e], kv_r.at[c, slot], clip_dev(e),
         )
 
     def project(x2):
@@ -248,11 +252,22 @@
             acc = dot(t, w_all[:, :, lo:hi].reshape(1024, hi - lo), 1, 0)
             kv_part[:, x2, :, lo:hi] = acc.astype(BF16).reshape(2, 128, hi - lo)
 
-    def kv_start(core, x2):
+    def kv_start(c, core, x2):
         e = core * 4 + x2
-        kv_copy(e, my_clip).start()
-        sends.append(lambda: kv_copy(e, my_clip).wait_send())
-
+        kv_copy(c, e, my_clip).start()
+        sends.append(lambda: kv_copy(c, e, my_clip).wait_send())
+
+    def kv_block(c, o):
+        x2 = lax.rem(x + o, 4)
+        cols = pl.ds(CUTS[c][0], CUTS[c][1] - CUTS[c][0])
+        if o == 0:
+            keep(f"kv{c}", local(kv_part.at[k, x, :, cols], kv_recv.at[k, x, :, cols], 14 + 2 * len(CUTS) + c))
+        else:
+            kv_start(c, k, x2)
+        kv_start(c, ek, x2)
+
+    held_parts = range(1, len(CUTS))
+    held = []
     for o in order:
         x2 = lax.rem(x + o, 4)
         arrive(f"t2_{o}")
@@ -263,12 +278,17 @@
             arrive("w_far1")
         arrive(f"t3_{o}")
         project(x2)
-        if o == 0:
-            keep("kv", local(kv_part.at[k, x], kv_recv.at[k, x], 10))
-        else:
-            kv_start(k, x2)
-        kv_start(ek, x2)
-    arrivals["kv"].append(lambda: others(8, my_clip, lambda e: kv_copy(e, e).wait_recv()))
+        kv_block(0, o)
+        for c in held_parts:
+            held.append((c, o))
+        if len(held) > HOLD * len(held_parts):
+            for c, o2 in held[: len(held_parts)]:
+                kv_block(c, o2)
+            held = held[len(held_parts) :]
+    for c, o2 in sorted(held):
+        kv_block(c, o2)
+    for c in range(len(CUTS)):
+        arrivals[f"kv{c}"].append(lambda c=c: others(8, my_clip, lambda e: kv_copy(c, e, e).wait_recv()))
 
     def turn(z2):
         text_t[z2] = text[:, :, :, rows_of(z2, 256)].reshape(1024, 256).T
@@ -281,6 +301,7 @@
 
     def gather_kv(c):
         lo, hi = CUTS[c]
+        arrive(f"kv{c}")
         for i in range(2):
             acc = kv_recv[i, 0, :, lo:hi].astype(F32)
             for b in range(1, 4):
@@ -339,7 +360,7 @@
         arrive(f"px{c}")
         gr_own[:, :, lo:hi] = (pg_own[:, :, lo:hi] + pg_recv[:, :, lo:hi].astype(F32)).astype(BF16)
         group(f"ga{c}", 8, my_clip, lambda e, slot: ga_copy(c, e, slot))
-        keep(f"ga{c}", local(gr_own.at[k, :, cols], gr_all.at[k, x, :, cols], 19 + c))
+        keep(f"ga{c}", local(gr_own.at[k, :, cols], gr_all.at[k, x, :, cols], 14 + c))
 
     def dw_copy(c, e, slot):
         cols = pl.ds(CUTS[c][0], CUTS[c][1] - CUTS[c][0])
@@ -377,7 +398,7 @@
             dw_send(c, near_row(o, 1 - i))
         step(z)
         dw_send(c, z * 2 + ek)
-        keep(f"dw{c}", local(dw_part.at[my_row, :, cols], dw_recv.at[k, z, :, cols], 22 + c))
+        keep(f"dw{c}", local(dw_part.at[my_row, :, cols], dw_recv.at[k, z, :, cols], 14 + len(CUTS) + c))
         arrivals[f"dw{c}"] += [
             lambda e=e: dw_copy(c, e, e).wait_recv()
             for e in [near_row(o, k2) for o, k2 in near] + [z * 2 + ek]
@@ -402,8 +423,6 @@
             out[:, lo:hi] = acc
 
     last = len(CUTS) - 1
-    arrive("kv")
-    gather_kv(0)
     arrive("mine")
 
     def heads_of(name, l2, c, kept):
@@ -411,27 +430,25 @@
             arrive(f"{name}_{c}_{i}")
         heads(l2, c, kept)
 
-    heads_of("own", l, 0, pg_own)
     for c in range(len(CUTS)):
-        if c < last:
-            gather_kv(c + 1)
-        if c == 0:
-            pass
+        gather_kv(c)
+        heads_of("own", l, c, pg_own)
+        if c > 0:
+            ga_start(c - 1)
         arrive(f"kx{c}")
         heads_of("far", el, c, pg_send)
         px_start(c)
-        if c < last:
-            heads_of("own", l, c + 1, pg_own)
-        if c == max(0, last - 1):
+        if c == last:
             oq_start("oq_own", l, 12)
-        if c == last:
             oq_start("oq_far", el, 13)
-        if c > 0:
-            dw_start(c - 1)
-        ga_start(c)
+            if last > 0:
+                dw_start(0)
+            ga_start(c)
+    for c in range(len(CUTS)):
+        if c > 0 or last == 0:
+            dw_start(c)
         if c > 0:
             dw_add(c - 1)
-    dw_start(last)
     dw_add(last)
     for c in range(len(CUTS)):
         dw_end(c)
@@ -442,6 +459,7 @@
     any_spec = pl.BlockSpec(memory_space=pl.ANY)
     vmem = pl.BlockSpec(memory_space=pltpu.VMEM)
     dma = pltpu.SemaphoreType.DMA
+    n = len(CUTS)
     scratch = [
         pltpu.VMEM((4, 32, 4096), BF16),
         pltpu.VMEM((32, 4096), BF16),
@@ -466,7 +484,7 @@
         pltpu.VMEM((8, 128, 640), BF16),
         pltpu.VMEM((2, 4, 128, 640), BF16),
         pltpu.VMEM((2, 128, 640), BF16),
-        dma((25,)),
+        dma((14 + 3 * n,)),
         dma((2, 4)), dma((2, 4)),
         dma((2,)), dma((2,)),
         dma((4,)), dma((4,)),
@@ -474,14 +492,14 @@
         dma((4,)), dma((4,)),
         dma((8,)), dma((8,)),
         dma((2,)), dma((2,)),
-        dma((8,)), dma((8,)),
-        dma((3,)), dma((3,)),
-        dma((2, 2, 3, 4)), dma((2, 2, 3, 4)),
-        dma((3,)), dma((3,)),
+        dma((n, 8)), dma((n, 8)),
+        dma((n,)), dma((n,)),
+        dma((2, 2, n, 4)), dma((2, 2, n, 4)),
+        dma((n,)), dma((n,)),
         dma((2, 4)), dma((2, 4)),
-        dma((3, 8)), dma((3, 8)),
-        dma((3, 8)), dma((3, 8)),
-        dma((3, 2)), dma((3, 2)),
+        dma((n, 8)), dma((n, 8)),
+        dma((n, 8)), dma((n, 8)),
+        dma((n, 2)), dma((n, 2)),
     ]
     return pl.pallas_call(
         kernel,

time: 117 us -> 110 us (0.940)
  Pallas kernels: 112 us -> 104 us
    pallas_call x1, Pallas kernels: 112 us -> 104 us  [on_device(): pl.pallas_call(kernel, out_shape=(jax.ShapeDtypeStruct(queries.shape, BF1...]
where the time goes in v4:
time: 110 us; the launch traced here: 109 us
  Pallas kernels  104 us (95%)
  local copies, waits for them, and re-layouts  3.98 us (4%)
    pallas_call x1, Pallas kernels, on_device(): pl.pallas_call(kernel, out_shape=(jax.ShapeDtypeStruct(queries.shape, BF1...  104 us
    unnamed x7, local copies, waits for them, and re-layouts  3.98 us

profile of v4, /device:TPU:1, one launch (start us, length us, event | category | flops | bytes accessed | tf_op | source)
XLA Modules:
  0.0 108.8 jit_solution(6399326482528885327)
XLA Ops:
  0.6 104.2 %shard_map.94 = (bf16[1,128,5120]{2,1,0:T(8,128)(2,1)}, f32[128,640]{1,0:T(8,128)}, f32[128,640]{1,0:T(8,128)}) custom-call(bf16[1,1,128,4096]{3,2,1,0:T(8,128)(2,1)} %enc.1, bf16[1,128,4096]{2,1,0:T(8,128)(2,1)} %resid.1, f32[1,4096]{1,0:T(1,128)} %bitcast.1, bf16[128,640]{1,0:T(8,128)(2,1)} %key_w.1, bf16[128,640]{1,0:T(8,128)(2,1)} %val_w.1, ...), custom_call_target="tpu_custom_call" | custom-call | flops 4000000000 | bytes 10000000 | tf_op jit(solution)/shard_map/pallas_call | solution.py:504
  104.8 0.0 copy-start.1
  104.8 0.0 copy-start
  104.8 2.5 %copy.13 = bf16[1,128,5120]{2,1,0:T(8,128)(2,1)} copy(bf16[1,128,5120]{2,1,0:T(8,128)(2,1)} %get-tuple-element.6) | data formatting | bytes 2621440
  107.4 0.0 copy-done.1
  107.4 0.7 copy.14
  108.1 0.0 copy-done
  108.1 0.7 copy.15
Async XLA Ops:
  104.8 2.5 %copy-start.1 = (f32[128,640]{1,0:T(8,128)S(1)}, f32[128,640]{1,0:T(8,128)}, u32[]{:S(2)}) copy-start(f32[128,640]{1,0:T(8,128)} %get-tuple-element.7) | copy-start | bytes 983044
  104.8 3.3 %copy-start = (f32[128,640]{1,0:T(8,128)S(1)}, f32[128,640]{1,0:T(8,128)}, u32[]{:S(2)}) copy-start(f32[128,640]{1,0:T(8,128)} %get-tuple-element.8) | copy-start | bytes 983044

commit v5 on v4

--- a/solution.py
+++ b/solution.py
@@ -183,6 +183,20 @@
         qg_start(name, l2, c)
     arrive("ez_0")
     arrive("ez_1")
+    arrive("w_near")
+
+    def w_pass(i):
+        o = (3, 1)[i]
+        part = w_all.at[pl.ds(lax.rem(z + o, 4) * 2, 2), pl.ds(64 * i, 64)]
+        return remote(part, part, wf_s.at[i], wf_r.at[i], device(x, lax.rem(z + 4 - o, 4), k, l, y))
+
+    def w_passed(i):
+        part = w_all.at[pl.ds(lax.rem(z + 2, 4) * 2, 2), pl.ds(64 * i, 64)]
+        return remote(part, part, wf_s.at[i], wf_r.at[i], device(x, lax.rem(z + 1, 4), k, l, y))
+
+    for i in range(2):
+        pair(f"w_far{i}", w_pass(i), w_passed(i))
+
 
     def hidden(b):
         cols = pl.ds(b * 1024, 1024)
@@ -204,20 +218,6 @@
     group("t1", 4, x, t1_copy)
     arrivals.pop("t1")
     keep("t1", local(text32.at[x], text.at[k, x, rows_of(y, 32)], 9))
-
-    arrive("w_near")
-
-    def w_pass(i):
-        o = (3, 1)[i]
-        part = w_all.at[pl.ds(lax.rem(z + o, 4) * 2, 2), pl.ds(64 * i, 64)]
-        return remote(part, part, wf_s.at[i], wf_r.at[i], device(x, lax.rem(z + 4 - o, 4), k, l, y))
-
-    def w_passed(i):
-        part = w_all.at[pl.ds(lax.rem(z + 2, 4) * 2, 2), pl.ds(64 * i, 64)]
-        return remote(part, part, wf_s.at[i], wf_r.at[i], device(x, lax.rem(z + 1, 4), k, l, y))
-
-    for i in range(2):
-        pair(f"w_far{i}", w_pass(i), w_passed(i))
 
     def t2_copy(x2, y2, slot):
         part = text.at[k, x2, rows_of(slot, 32)]

time: 110 us -> 109 us (level)
  no operation moved by 1% of the time
where the time goes in v5:
time: 109 us; the launch traced here: 108 us
  Pallas kernels  103 us (94%)
  local copies, waits for them, and re-layouts  3.98 us (4%)
    pallas_call x1, Pallas kernels, on_device(): pl.pallas_call(kernel, out_shape=(jax.ShapeDtypeStruct(queries.shape, BF1...  103 us
    unnamed x7, local copies, waits for them, and re-layouts  3.98 us

profile of v5, /device:TPU:1, one launch (start us, length us, event | category | flops | bytes accessed | tf_op | source)
XLA Modules:
  0.0 107.9 jit_solution(9717141945240139097)
XLA Ops:
  0.6 103.3 %shard_map.94 = (bf16[1,128,5120]{2,1,0:T(8,128)(2,1)}, f32[128,640]{1,0:T(8,128)}, f32[128,640]{1,0:T(8,128)}) custom-call(bf16[1,1,128,4096]{3,2,1,0:T(8,128)(2,1)} %enc.1, bf16[1,128,4096]{2,1,0:T(8,128)(2,1)} %resid.1, f32[1,4096]{1,0:T(1,128)} %bitcast.1, bf16[128,640]{1,0:T(8,128)(2,1)} %key_w.1, bf16[128,640]{1,0:T(8,128)(2,1)} %val_w.1, ...), custom_call_target="tpu_custom_call" | custom-call | flops 4000000000 | bytes 10000000 | tf_op jit(solution)/shard_map/pallas_call | solution.py:504
  103.9 0.0 copy-start.1
  103.9 0.0 copy-start
  103.9 2.5 %copy.13 = bf16[1,128,5120]{2,1,0:T(8,128)(2,1)} copy(bf16[1,128,5120]{2,1,0:T(8,128)(2,1)} %get-tuple-element.6) | data formatting | bytes 2621440
  106.4 0.0 copy-done.1
  106.4 0.7 copy.14
  107.2 0.0 copy-done
  107.2 0.7 copy.15
Async XLA Ops:
  103.9 2.5 %copy-start.1 = (f32[128,640]{1,0:T(8,128)S(1)}, f32[128,640]{1,0:T(8,128)}, u32[]{:S(2)}) copy-start(f32[128,640]{1,0:T(8,128)} %get-tuple-element.7) | copy-start | bytes 983044
  103.9 3.3 %copy-start = (f32[128,640]{1,0:T(8,128)S(1)}, f32[128,640]{1,0:T(8,128)}, u32[]{:S(2)}) copy-start(f32[128,640]{1,0:T(8,128)} %get-tuple-element.8) | copy-start | bytes 983044

commit v6 on v5

--- a/solution.py
+++ b/solution.py
@@ -439,11 +439,11 @@
         heads_of("far", el, c, pg_send)
         px_start(c)
         if c == last:
-            oq_start("oq_own", l, 12)
-            oq_start("oq_far", el, 13)
             if last > 0:
                 dw_start(0)
             ga_start(c)
+            oq_start("oq_own", l, 12)
+            oq_start("oq_far", el, 13)
     for c in range(len(CUTS)):
         if c > 0 or last == 0:
             dw_start(c)

time: 109 us -> 109 us (level)
  no operation moved by 1% of the time
where the time goes in v6:
time: 109 us; the launch traced here: 108 us
  Pallas kernels  104 us (95%)
  local copies, waits for them, and re-layouts  3.98 us (4%)
    pallas_call x1, Pallas kernels, on_device(): pl.pallas_call(kernel, out_shape=(jax.ShapeDtypeStruct(queries.shape, BF1...  104 us
    unnamed x7, local copies, waits for them, and re-layouts  3.98 us

profile of v6, /device:TPU:1, one launch (start us, length us, event | category | flops | bytes accessed | tf_op | source)
XLA Modules:
  0.0 108.5 jit_solution(2485847314423623971)
XLA Ops:
  0.6 103.8 %shard_map.94 = (bf16[1,128,5120]{2,1,0:T(8,128)(2,1)}, f32[128,640]{1,0:T(8,128)}, f32[128,640]{1,0:T(8,128)}) custom-call(bf16[1,1,128,4096]{3,2,1,0:T(8,128)(2,1)} %enc.1, bf16[1,128,4096]{2,1,0:T(8,128)(2,1)} %resid.1, f32[1,4096]{1,0:T(1,128)} %bitcast.1, bf16[128,640]{1,0:T(8,128)(2,1)} %key_w.1, bf16[128,640]{1,0:T(8,128)(2,1)} %val_w.1, ...), custom_call_target="tpu_custom_call" | custom-call | flops 4000000000 | bytes 10000000 | tf_op jit(solution)/shard_map/pallas_call | solution.py:504
  104.5 0.0 copy-start.1
  104.5 0.0 copy-start
  104.5 2.5 %copy.13 = bf16[1,128,5120]{2,1,0:T(8,128)(2,1)} copy(bf16[1,128,5120]{2,1,0:T(8,128)(2,1)} %get-tuple-element.6) | data formatting | bytes 2621440
  107.0 0.0 copy-done.1
  107.0 0.7 copy.14
  107.8 0.0 copy-done
  107.8 0.7 copy.15
Async XLA Ops:
  104.5 2.5 %copy-start.1 = (f32[128,640]{1,0:T(8,128)S(1)}, f32[128,640]{1,0:T(8,128)}, u32[]{:S(2)}) copy-start(f32[128,640]{1,0:T(8,128)} %get-tuple-element.7) | copy-start | bytes 983044
  104.5 3.3 %copy-start = (f32[128,640]{1,0:T(8,128)S(1)}, f32[128,640]{1,0:T(8,128)}, u32[]{:S(2)}) copy-start(f32[128,640]{1,0:T(8,128)} %get-tuple-element.8) | copy-start | bytes 983044
